TPU v7x, 32 devices: a whole 2x2x4 slice. The times are simulated.
32 devices in a mesh: expert: 8 (over z, x), shard: 4 (over y, core).
Axes of the slice: x: 2, y: 2, z: 4, core: 2. Of those that a mesh axis runs over, the one named last changes fastest.
Arguments:
- tokens: bfloat16 [2, 4096, 768], P(None, ('expert', 'shard')), may hold values from -6 to 6
- cotangent: bfloat16 [2, 4096, 768], P(None, ('expert', 'shard')), may hold values from -6 to 6
- routes: int32 [2, 4096, 2], P(None, ('expert', 'shard')), may hold values from 0 to 15, all different within a row; in each aligned block of 128 rows (0 to 127, 128 to 255, ..., all dimensions but the last counted through in order) at most 18 rows name the same one
- prompt_rows: int32 [2, 8, 4], P(None, 'expert'), may hold values from 1 to 96, 256 in all within a row
- w_query: bfloat16 [768, 768], P('shard'), may hold values from -0.21875 to 0.21875
- w_key: bfloat16 [768, 768], P('shard'), may hold values from -0.21875 to 0.21875
- w_value: bfloat16 [768, 768], P('shard'), may hold values from -0.21875 to 0.21875
- w_output: bfloat16 [768, 768], P('shard'), may hold values from -3.5 to 3.5
- w_router: bfloat16 [768, 16], P('shard'), may hold values from -0.15625 to 0.15625
- gain_attn: bfloat16 [768], P('shard'), may hold values from 0.099609375 to 1.8984375
- gain_ffn: bfloat16 [768], P('shard'), may hold values from 0.099609375 to 1.8984375
- pos_table: bfloat16 [384], P('shard'), may hold values from -4 to 4
- w_in: bfloat16 [16, 768, 3072], P('expert', None, 'shard'), may hold values from -0.21875 to 0.21875
- w_out: bfloat16 [16, 3072, 768], P('expert', 'shard'), may hold values from -0.109375 to 0.109375
Outputs:
- mixed: bfloat16 [2, 4096, 768], P(None, ('expert', 'shard'))
- d_tokens: float32 [2, 4096, 768], P(None, ('expert', 'shard'))
- d_query: float32 [768, 768], P('shard')
- d_key: float32 [768, 768], P('shard')
- d_value: float32 [768, 768], P('shard')
- d_output: float32 [768, 768], P('shard')
- d_router: float32 [768, 16], P('shard')
- d_gain_attn: float32 [768], P('shard')
- d_gain_ffn: float32 [768], P('shard')
- d_table: float32 [384], P('shard')
- d_in: float32 [16, 768, 3072], P('expert', None, 'shard')
- d_out: float32 [16, 3072, 768], P('expert', 'shard')
Inputs may be any that keep to these rules, and one draw needn't show every extreme that they name: `routes`: each row names two different experts. In each micro-batch, the 128 rows of one device name no expert more than 18 times, a bound that some block reaches. `prompt_rows`: the 4 counts of a group sum to 256; the largest is exactly 96.
All inputs are finite; a program needn't handle non-finite values.
Results may differ from a plain program's by a relative error of at most 0.02.
Values may be sent and summed in bfloat16 or wider, within the bound.
A program may use at most 192 MiB of HBM per device.

v0:
```python
from functools import reduce
import math

import jax
import jax.numpy as jnp
from jax import lax
from jax.sharding import PartitionSpec as P

HEADS = 12
BUCKETS = 32


EPS = 1e-06
MASKED = -1e30
BUCKET_EDGES = (24, 32, 48, 64, 96, 128, 192, 256, 384, 512, 768, 1024, 1536, 2048, 3072)
HIGHEST = lax.Precision.HIGHEST


def distance_bucket(distance):
    coarse = reduce(
        lambda running, border: running + (distance >= border).astype(jnp.int32),
        BUCKET_EDGES,
        jnp.full(distance.shape, 16, jnp.int32),
    )
    return jnp.where(distance < 16, distance, coarse)


def layout(counts, block_rows):
    shard_count = counts.shape[0]
    offsets = jnp.cumsum(counts, dtype=jnp.int32) - counts
    row_index = jnp.arange(shard_count * block_rows, dtype=jnp.int32)
    device = row_index // block_rows
    local_row = row_index - device * block_rows
    own_count = counts[device]
    is_prompt = local_row < own_count
    prompt_total = jnp.sum(counts, dtype=jnp.int32)
    position = jnp.where(
        is_prompt, offsets[device] + local_row, prompt_total + local_row - own_count
    )
    return (position, is_prompt, device)


def rms_norm(values, gain):
    return values * lax.rsqrt(jnp.mean(values * values, axis=-1, keepdims=True) + EPS) * gain


def matmul(left, right):
    return jnp.dot(left, right, preferred_element_type=jnp.float32)


def matmul_left(left, right):
    return lax.dot_general(
        left, right, (((0,), (0,)), ((), ())), preferred_element_type=jnp.float32
    )


def matmul_right(left, right):
    return lax.dot_general(
        left, right, (((1,), (1,)), ((), ())), preferred_element_type=jnp.float32
    )


def per_device(
    tokens,
    cotangent,
    routes,
    prompt_rows,
    w_query,
    w_key,
    w_value,
    w_output,
    w_router,
    gain_attn,
    gain_ffn,
    pos_table,
    w_in,
    w_out,
):
    shard_count = lax.axis_size("shard")
    expert_ranks = lax.axis_size("expert")
    own_index = lax.axis_index("shard")
    micro_count, tok_rows, model_width = tokens.shape
    local_experts = w_in.shape[0]
    expert_count = w_router.shape[1]
    capacity = (9 * tok_rows + 4 * expert_count - 1) // (4 * expert_count)
    head_count = HEADS
    head_size = model_width // head_count
    bucket_count = BUCKETS
    score_scale = head_size ** (-0.5)
    group_rows = shard_count * tok_rows
    slot_count = expert_ranks * capacity * local_experts
    recv_rows = expert_ranks * capacity
    bucket_ids = jnp.arange(bucket_count, dtype=jnp.int32)
    expert_ids = jnp.arange(expert_count, dtype=jnp.int32)
    gathered = (
        lax.all_gather(w_query, "shard", axis=0, tiled=True),
        lax.all_gather(w_key, "shard", axis=0, tiled=True),
        lax.all_gather(w_value, "shard", axis=0, tiled=True),
        lax.all_gather(w_output, "shard", axis=0, tiled=True),
        lax.all_gather(w_router, "shard", axis=0, tiled=True),
        lax.all_gather(gain_attn, "shard", axis=0, tiled=True),
        lax.all_gather(gain_ffn, "shard", axis=0, tiled=True),
        lax.all_gather(pos_table, "shard", axis=0, tiled=True),
    )
    full_query, full_key, full_value, full_output, full_router, gain_one, gain_two, table_flat = (
        gathered
    )
    gain_first = gain_one.astype(jnp.float32)
    gain_second = gain_two.astype(jnp.float32)
    table = table_flat.astype(jnp.float32).reshape(head_count, bucket_count)
    expert_in, expert_out = (
        lax.all_gather(w_in, "shard", axis=2, tiled=True),
        lax.all_gather(w_out, "shard", axis=1, tiled=True),
    )
    sum_query = jnp.zeros(full_query.shape, jnp.float32)
    sum_key = jnp.zeros(full_key.shape, jnp.float32)
    sum_value = jnp.zeros(full_value.shape, jnp.float32)
    sum_output = jnp.zeros(full_output.shape, jnp.float32)
    sum_router = jnp.zeros(full_router.shape, jnp.float32)
    sum_gain_one = jnp.zeros((model_width,), jnp.float32)
    sum_gain_two = jnp.zeros((model_width,), jnp.float32)
    sum_table = jnp.zeros((head_count, bucket_count), jnp.float32)
    sum_expert_in = jnp.zeros(expert_in.shape, jnp.float32)
    sum_expert_out = jnp.zeros(expert_out.shape, jnp.float32)
    mixed_parts = []
    grad_parts = []
    for micro_index in range(micro_count):
        inputs = tokens[micro_index].astype(jnp.float32)
        counts = prompt_rows[micro_index, 0]
        pos_all, prompt_all, device_all = layout(counts, tok_rows)
        query_pos = lax.dynamic_slice_in_dim(pos_all, own_index * tok_rows, tok_rows)
        hidden = rms_norm(inputs, gain_first).astype(jnp.bfloat16)
        query = matmul(hidden, full_query).astype(jnp.bfloat16)
        key = matmul(hidden, full_key).astype(jnp.bfloat16)
        value = matmul(hidden, full_value).astype(jnp.bfloat16)
        keys_all, values_all = (
            lax.all_gather(key, "shard", axis=0, tiled=True),
            lax.all_gather(value, "shard", axis=0, tiled=True),
        )
        key_index = jnp.arange(group_rows, dtype=jnp.int32)
        key_far = jnp.zeros((group_rows,), jnp.bool_)
        key_total = keys_all.shape[0]
        key_block = math.gcd(key_total, 512)
        block_count = key_total // key_block
        key_pos = pos_all[key_index]
        key_prompt = prompt_all[key_index]
        key_device = device_all[key_index]
        key_mine = key_device == own_index
        distance = query_pos[:, None] - key_pos[None, :]
        visible = (
            (distance >= 0)
            & (key_prompt | key_mine)[None, :]
            & jnp.logical_not(key_far & key_mine)[None, :]
        )
        bucket_all = distance_bucket(jnp.maximum(distance, 0))
        bucket_blocks = bucket_all.reshape(tok_rows, block_count, key_block).transpose(1, 0, 2)
        visible_blocks = visible.reshape(tok_rows, block_count, key_block).transpose(1, 0, 2)
        query_heads = query.reshape(tok_rows, head_count, head_size)
        key_blocks = keys_all.reshape(block_count, key_block, head_count, head_size)
        value_blocks = values_all.reshape(block_count, key_block, head_count, head_size)

        def make_bias(unused, block_item):
            bucket_piece, visible_piece = block_item
            bucket_hits = (bucket_piece[:, :, None] == bucket_ids).astype(jnp.float32)
            bias = jnp.einsum("qkb,hb->hqk", bucket_hits, table, precision=HIGHEST)
            return (unused, jnp.where(visible_piece[None], bias, MASKED))

        _, bias_blocks = lax.scan(
            make_bias, jnp.zeros((), jnp.float32), (bucket_blocks, visible_blocks)
        )

        def score_piece(key_piece, bias_piece):
            raw = jnp.einsum(
                "qhd,khd->hqk", query_heads, key_piece, preferred_element_type=jnp.float32
            )
            return raw * score_scale + bias_piece

        def running(state_pair, block_item):
            running_max, running_sum = state_pair
            key_piece, bias_piece = block_item
            scores = score_piece(key_piece, bias_piece)
            new_max = jnp.maximum(running_max, jnp.max(scores, axis=-1))
            running_sum = running_sum * jnp.exp(running_max - new_max) + jnp.sum(
                jnp.exp(scores - new_max[:, :, None]), axis=-1
            )
            return ((new_max, running_sum), None)

        start_pair = (
            jnp.full((head_count, tok_rows), MASKED, jnp.float32),
            jnp.zeros((head_count, tok_rows), jnp.float32),
        )
        (running_max, running_sum), _ = lax.scan(running, start_pair, (key_blocks, bias_blocks))
        log_total = running_max + jnp.log(running_sum)

        def gather_context(context_sum, block_item):
            key_piece, value_piece, bias_piece = block_item
            weights_low = jnp.exp(
                score_piece(key_piece, bias_piece) - log_total[:, :, None]
            ).astype(jnp.bfloat16)
            return (
                context_sum
                + jnp.einsum(
                    "hqk,khd->qhd", weights_low, value_piece, preferred_element_type=jnp.float32
                ),
                None,
            )

        context, _ = lax.scan(
            gather_context,
            jnp.zeros((tok_rows, head_count, head_size), jnp.float32),
            (key_blocks, value_blocks, bias_blocks),
        )
        context_low = context.reshape(tok_rows, model_width).astype(jnp.bfloat16)
        middle = inputs + matmul(context_low, full_output)
        normed = rms_norm(middle, gain_second).astype(jnp.bfloat16)
        logits = matmul(normed, full_router)
        chosen = routes[micro_index]
        pick_table = (chosen[:, :, None] == expert_ids).astype(jnp.float32)
        picked = jnp.sum(pick_table * logits[:, None, :], axis=-1)
        gate_weights = jax.nn.softmax(picked, axis=-1)
        flat_routes = chosen.reshape(-1)
        expert_hits = (flat_routes[:, None] == expert_ids).astype(jnp.int32)
        expert_rank = (
            jnp.sum(
                jnp.cumsum(expert_hits, axis=0, dtype=jnp.int32) * expert_hits,
                axis=1,
                dtype=jnp.int32,
            )
            - 1
        )
        slot_index = (
            flat_routes // local_experts * (capacity * local_experts)
            + expert_rank * local_experts
            + flat_routes % local_experts
        )
        slot_owner = (
            jnp.full((slot_count,), 2 * tok_rows, jnp.int32)
            .at[slot_index]
            .set(jnp.arange(2 * tok_rows, dtype=jnp.int32))
        )
        padded = jnp.concatenate([normed, jnp.zeros((1, model_width), jnp.bfloat16)], axis=0)
        outgoing = padded[slot_owner // 2].reshape(
            expert_ranks, capacity, local_experts, model_width
        )
        received = lax.all_to_all(
            outgoing, "expert", split_axis=0, concat_axis=0, tiled=True
        ).reshape(recv_rows, local_experts, model_width)
        pre_act = jnp.einsum(
            "red,edf->ref", received, expert_in, preferred_element_type=jnp.float32
        )
        activation = jax.nn.gelu(pre_act).astype(jnp.bfloat16)
        expert_result = jnp.einsum(
            "ref,efd->red", activation, expert_out, preferred_element_type=jnp.float32
        )
        result_low = expert_result.astype(jnp.bfloat16).reshape(
            expert_ranks, capacity, local_experts, model_width
        )
        returned = lax.all_to_all(
            result_low, "expert", split_axis=0, concat_axis=0, tiled=True
        ).reshape(slot_count, model_width)
        picked_rows = returned[slot_index].astype(jnp.float32).reshape(tok_rows, 2, model_width)
        output_rows = middle + jnp.sum(gate_weights[:, :, None] * picked_rows, axis=1)
        mixed_parts.append(output_rows.astype(jnp.bfloat16))
        grad_output = cotangent[micro_index].astype(jnp.float32)
        grad_gate = jnp.sum(grad_output[:, None, :] * picked_rows, axis=-1)
        grad_pick = gate_weights * (
            grad_gate - jnp.sum(gate_weights * grad_gate, axis=-1, keepdims=True)
        )
        grad_logits = jnp.sum(pick_table * grad_pick[:, :, None], axis=1).astype(jnp.bfloat16)
        sum_router = sum_router + matmul_left(normed, grad_logits)
        grad_normed = matmul_right(grad_logits, full_router)
        branch_grad = (gate_weights[:, :, None] * grad_output[:, None, :]).reshape(
            2 * tok_rows, model_width
        )
        padded_grad = jnp.concatenate(
            [branch_grad, jnp.zeros((1, model_width), jnp.float32)], axis=0
        )
        grad_send = (
            padded_grad[slot_owner]
            .astype(jnp.bfloat16)
            .reshape(expert_ranks, capacity, local_experts, model_width)
        )
        grad_recv = lax.all_to_all(
            grad_send, "expert", split_axis=0, concat_axis=0, tiled=True
        ).reshape(recv_rows, local_experts, model_width)
        grad_act = jnp.einsum(
            "red,efd->ref", grad_recv, expert_out, preferred_element_type=jnp.float32
        )
        sum_expert_out = sum_expert_out + jnp.einsum(
            "ref,red->efd", activation, grad_recv, preferred_element_type=jnp.float32
        )
        _, gelu_pull = jax.vjp(jax.nn.gelu, pre_act)
        grad_pre = gelu_pull(grad_act)[0].astype(jnp.bfloat16)
        sum_expert_in = sum_expert_in + jnp.einsum(
            "red,ref->edf", received, grad_pre, preferred_element_type=jnp.float32
        )
        grad_in_rows = jnp.einsum(
            "ref,edf->red", grad_pre, expert_in, preferred_element_type=jnp.float32
        )
        grad_in_low = grad_in_rows.astype(jnp.bfloat16).reshape(
            expert_ranks, capacity, local_experts, model_width
        )
        grad_back = lax.all_to_all(
            grad_in_low, "expert", split_axis=0, concat_axis=0, tiled=True
        ).reshape(slot_count, model_width)
        grad_normed = grad_normed + jnp.sum(
            grad_back[slot_index].astype(jnp.float32).reshape(tok_rows, 2, model_width), axis=1
        )
        _, norm_pull = jax.vjp(rms_norm, middle, gain_second)
        grad_middle, grad_gain_second = norm_pull(grad_normed)
        grad_middle = grad_middle + grad_output
        sum_gain_two = sum_gain_two + grad_gain_second
        grad_attn = grad_middle.astype(jnp.bfloat16)
        sum_output = sum_output + matmul_left(context_low, grad_attn)
        grad_context = (
            matmul_right(grad_attn, full_output)
            .astype(jnp.bfloat16)
            .reshape(tok_rows, head_count, head_size)
        )
        row_delta = jnp.einsum("qhd,qhd->hq", grad_context.astype(jnp.float32), context)

        def attend_back(state_pair, block_item):
            grad_query_sum, grad_table_sum = state_pair
            key_piece, value_piece, bias_piece, bucket_piece = block_item
            probs = jnp.exp(score_piece(key_piece, bias_piece) - log_total[:, :, None])
            grad_probs = jnp.einsum(
                "qhd,khd->hqk", grad_context, value_piece, preferred_element_type=jnp.float32
            )
            grad_scores = probs * (grad_probs - row_delta[:, :, None])
            bucket_hits = (bucket_piece[:, :, None] == bucket_ids).astype(jnp.float32)
            grad_table_sum = grad_table_sum + jnp.einsum(
                "hqk,qkb->hb", grad_scores, bucket_hits, precision=HIGHEST
            )
            grad_raw = (grad_scores * score_scale).astype(jnp.bfloat16)
            grad_query_sum = grad_query_sum + jnp.einsum(
                "hqk,khd->qhd", grad_raw, key_piece, preferred_element_type=jnp.float32
            )
            grad_key_piece = jnp.einsum(
                "hqk,qhd->khd", grad_raw, query_heads, preferred_element_type=jnp.float32
            )
            grad_value_piece = jnp.einsum(
                "hqk,qhd->khd",
                probs.astype(jnp.bfloat16),
                grad_context,
                preferred_element_type=jnp.float32,
            )
            return ((grad_query_sum, grad_table_sum), (grad_key_piece, grad_value_piece))

        back_start = (
            jnp.zeros((tok_rows, head_count, head_size), jnp.float32),
            jnp.zeros((head_count, bucket_count), jnp.float32),
        )
        (grad_query_all, grad_table_all), (grad_key_blocks, grad_value_blocks) = lax.scan(
            attend_back, back_start, (key_blocks, value_blocks, bias_blocks, bucket_blocks)
        )
        sum_table = sum_table + grad_table_all
        key_grad_rows = grad_key_blocks.reshape(key_total, model_width)
        value_grad_rows = grad_value_blocks.reshape(key_total, model_width)
        own_key_grad, own_value_grad = (
            lax.psum_scatter(
                key_grad_rows.astype(jnp.bfloat16), "shard", scatter_dimension=0, tiled=True
            ).astype(jnp.float32),
            lax.psum_scatter(
                value_grad_rows.astype(jnp.bfloat16), "shard", scatter_dimension=0, tiled=True
            ).astype(jnp.float32),
        )
        grad_query_low = grad_query_all.reshape(tok_rows, model_width).astype(jnp.bfloat16)
        grad_key_low = own_key_grad.astype(jnp.bfloat16)
        grad_value_low = own_value_grad.astype(jnp.bfloat16)
        sum_query = sum_query + matmul_left(hidden, grad_query_low)
        sum_key = sum_key + matmul_left(hidden, grad_key_low)
        sum_value = sum_value + matmul_left(hidden, grad_value_low)
        grad_hidden = (
            matmul_right(grad_query_low, full_query)
            + matmul_right(grad_key_low, full_key)
            + matmul_right(grad_value_low, full_value)
        )
        _, first_pull = jax.vjp(rms_norm, inputs, gain_first)
        grad_inputs, grad_gain_first = first_pull(grad_hidden)
        sum_gain_one = sum_gain_one + grad_gain_first
        grad_parts.append(grad_inputs + grad_middle)
    shares = (
        lax.psum_scatter(
            sum_query.astype(jnp.bfloat16), "shard", scatter_dimension=0, tiled=True
        ).astype(jnp.float32),
        lax.psum_scatter(
            sum_key.astype(jnp.bfloat16), "shard", scatter_dimension=0, tiled=True
        ).astype(jnp.float32),
        lax.psum_scatter(
            sum_value.astype(jnp.bfloat16), "shard", scatter_dimension=0, tiled=True
        ).astype(jnp.float32),
        lax.psum_scatter(
            sum_output.astype(jnp.bfloat16), "shard", scatter_dimension=0, tiled=True
        ).astype(jnp.float32),
        lax.psum_scatter(
            sum_router.astype(jnp.bfloat16), "shard", scatter_dimension=0, tiled=True
        ).astype(jnp.float32),
        lax.psum_scatter(
            sum_gain_one.astype(jnp.bfloat16), "shard", scatter_dimension=0, tiled=True
        ).astype(jnp.float32),
        lax.psum_scatter(
            sum_gain_two.astype(jnp.bfloat16), "shard", scatter_dimension=0, tiled=True
        ).astype(jnp.float32),
        lax.psum_scatter(
            sum_table.reshape(-1).astype(jnp.bfloat16), "shard", scatter_dimension=0, tiled=True
        ).astype(jnp.float32),
    )
    own_grads = (
        lax.psum(shares[0].astype(jnp.bfloat16), "expert").astype(jnp.float32),
        lax.psum(shares[1].astype(jnp.bfloat16), "expert").astype(jnp.float32),
        lax.psum(shares[2].astype(jnp.bfloat16), "expert").astype(jnp.float32),
        lax.psum(shares[3].astype(jnp.bfloat16), "expert").astype(jnp.float32),
        lax.psum(shares[4].astype(jnp.bfloat16), "expert").astype(jnp.float32),
        lax.psum(shares[5].astype(jnp.bfloat16), "expert").astype(jnp.float32),
        lax.psum(shares[6].astype(jnp.bfloat16), "expert").astype(jnp.float32),
        lax.psum(shares[7].astype(jnp.bfloat16), "expert").astype(jnp.float32),
    )
    grad_expert_in, grad_expert_out = (
        lax.psum_scatter(
            sum_expert_in.astype(jnp.bfloat16), "shard", scatter_dimension=2, tiled=True
        ).astype(jnp.float32),
        lax.psum_scatter(
            sum_expert_out.astype(jnp.bfloat16), "shard", scatter_dimension=1, tiled=True
        ).astype(jnp.float32),
    )
    return (
        jnp.stack(mixed_parts),
        jnp.stack(grad_parts),
        own_grads[0],
        own_grads[1],
        own_grads[2],
        own_grads[3],
        own_grads[4],
        own_grads[5],
        own_grads[6],
        own_grads[7],
        grad_expert_in,
        grad_expert_out,
    )


def solution(mesh):
    in_specs = (
        P(None, ("expert", "shard"), None),
        P(None, ("expert", "shard"), None),
        P(None, ("expert", "shard"), None),
        P(None, "expert", None),
        P("shard", None),
        P("shard", None),
        P("shard", None),
        P("shard", None),
        P("shard", None),
        P("shard"),
        P("shard"),
        P("shard"),
        P("expert", None, "shard"),
        P("expert", "shard", None),
    )
    out_specs = (
        P(None, ("expert", "shard"), None),
        P(None, ("expert", "shard"), None),
        P("shard", None),
        P("shard", None),
        P("shard", None),
        P("shard", None),
        P("shard", None),
        P("shard"),
        P("shard"),
        P("shard"),
        P("expert", None, "shard"),
        P("expert", "shard", None),
    )
    return jax.shard_map(
        per_device, mesh=mesh, in_specs=in_specs, out_specs=out_specs, check_vma=False
    )
```

profile of v0, /device:TPU:0, one launch (start us, length us, event | category | flops | bytes accessed | tf_op | source)
XLA Modules:
  0.0 878.3 jit_solution(5068343035857618702)
XLA Ops:
  26.5 3.5 gather_fusion
  30.1 3.5 gather_fusion.5
  37.3 8.9 %all-reduce.13 = (bf16[768]{0:T(1024)(128)(2,1)S(1)}, bf16[384]{0:T(512)(128)(2,1)S(1)}, bf16[768]{0:T(1024)(128)(2,1)S(1)}) all-reduce(bf16[768]{0:T(1024)(128)(2,1)S(1)} %dynamic-update-slice, bf16[384]{0:T(512)(128)(2,1)S(1)} %dynamic-update-slice.1, ...), channel_id=1, replica_groups=mesh['expert'=8,'shard'=4] {'shard'}, use_global_device_ids=true, to_apply=%add.4 | all-reduce | flops 1920 | bytes 7680
  46.3 3.5 gather_fusion.2
  49.9 3.4 gather_fusion.1
  53.2 3.4 gather_fusion.6
  56.6 5.4 all-gather
  69.9 3.4 fusion.1
  73.3 5.0 copy.204
  78.3 3.4 fusion.3
  81.6 4.9 copy.190
  101.9 13.4 %all_gather.44 = bf16[512,768]{1,0:T(8,128)(2,1)S(1)} all-gather(bf16[128,768]{1,0:T(8,128)(2,1)S(1)} %convolution_convert_fusion.17), channel_id=1, replica_groups=mesh['expert'=8,'shard'=4] {'shard'}, dimensions={0}, use_global_device_ids=true | all-gather | bytes 983040 | tf_op jit(solution)/shard_map/all_gather | solution.py:138
  118.2 13.7 %all_gather.55 = bf16[512,768]{1,0:T(8,128)(2,1)S(1)} all-gather(bf16[128,768]{1,0:T(8,128)(2,1)S(1)} %convolution_convert_fusion.12), channel_id=1, replica_groups=mesh['expert'=8,'shard'=4] {'shard'}, dimensions={0}, use_global_device_ids=true | all-gather | bytes 983040 | tf_op jit(solution)/shard_map/all_gather | solution.py:137
  133.4 13.3 %all_gather.54 = bf16[512,768]{1,0:T(8,128)(2,1)S(1)} all-gather(bf16[128,768]{1,0:T(8,128)(2,1)S(1)} %convolution_convert_fusion.14), channel_id=1, replica_groups=mesh['expert'=8,'shard'=4] {'shard'}, dimensions={0}, use_global_device_ids=true | all-gather | bytes 983040 | tf_op jit(solution)/shard_map/all_gather | solution.py:138
  147.4 13.3 %all_gather.47 = bf16[512,768]{1,0:T(8,128)(2,1)S(1)} all-gather(bf16[128,768]{1,0:T(8,128)(2,1)S(1)} %convolution_convert_fusion.15), channel_id=1, replica_groups=mesh['expert'=8,'shard'=4] {'shard'}, dimensions={0}, use_global_device_ids=true | all-gather | bytes 983040 | tf_op jit(solution)/shard_map/all_gather | solution.py:137
  161.0 3.1 fusion.186
  178.0 5.9 all-to-all-start
  183.9 3.0 fusion.187
  191.3 5.9 all-to-all-done
  197.2 4.1 all-to-all-start.4
  201.3 7.1 convolution_bitcast_fusion.3
  208.4 27.1 %all-gather.18.cloned.1.call-done = bf16[2,3072,768]{2,1,0:T(8,128)(2,1)} async-done(((bf16[2,768,768]{2,1,0:T(8,128)(2,1)}), bf16[2,3072,768]{2,1,0:T(8,128)(2,1)}) %all-gather.18.cloned.1.call-update) | async-done | bytes 9437200 | tf_op jit(solution)/shard_map/all_gather | solution.py:113
  235.5 6.7 fusion.24
  243.3 5.5 all-to-all-start.1
  248.9 8.8 %fusion.14 = bf16[144,2,3072]{2,0,1:T(8,128)(2,1)S(1)} fusion(f32[144,2,3072]{2,0,1:T(8,128)} %convolution_bitcast_fusion.3, bf16[2,3072,768]{2,1,0:T(8,128)(2,1)} %all-gather.18.cloned.1.call-done, bf16[144,2,768]{2,1,0:T(2,128)(2,1)} %bitcast.367), kind=kOutput, calls=%fused_computation.41 | convolution fusion | flops 1376649216 | bytes 15187968 | tf_op jit(solution)/shard_map/red,efd->ref/dot_general | solution.py:286
  257.7 3.2 fusion.26
  262.1 6.3 all-to-all-start.5
  273.5 7.5 all-to-all-done.5
  288.5 3.6 all-to-all-start.2
  295.9 8.9 %all-to-all-done.2 = bf16[8,18,2,768]{3,2,1,0:T(2,128)(2,1)S(1)} async-done(((bf16[8,18,2,768]{3,2,1,0:T(2,128)(2,1)}), bf16[8,18,2,768]{3,2,1,0:T(2,128)(2,1)S(1)}, u32[]{:S(2)}, u32[]{:S(2)}) %all-to-all-start.2) | async-done | bytes 442400 | tf_op jit(solution)/shard_map/all_to_all | solution.py:245
  304.7 3.6 all-to-all-start.6
  308.4 5.2 convolution_bitcast_fusion.2
  313.6 7.0 fusion.25
  321.7 6.2 all-to-all-start.3
  328.0 10.4 %fusion.21 = bf16[144,2,3072]{2,0,1:T(8,128)(2,1)S(1)} fusion(f32[144,2,3072]{2,0,1:T(8,128)} %copy-done.9, bf16[2,3072,768]{2,1,0:T(8,128)(2,1)} %all-gather.18.cloned.1.call-done, bf16[144,2,768]{2,1,0:T(2,128)(2,1)S(1)} %bitcast.369), kind=kOutput, calls=%fused_computation.48 | convolution fusion | flops 1376649216 | bytes 15187968 | tf_op jit(solution)/shard_map/red,efd->ref/dot_general | solution.py:286
  338.4 7.7 fusion.27
  347.2 6.0 all-to-all-start.7
  355.2 9.5 %all-to-all-done.7 = bf16[8,18,2,768]{3,2,1,0:T(2,128)(2,1)S(1)} async-done(((bf16[8,18,2,768]{3,2,1,0:T(2,128)(2,1)}), bf16[8,18,2,768]{3,2,1,0:T(2,128)(2,1)S(1)}, u32[]{:S(2)}, u32[]{:S(2)}) %all-to-all-start.7) | async-done | bytes 442400 | tf_op jit(solution)/shard_map/all_to_all | solution.py:303
  389.9 3.7 convolution_convert_fusion
  420.8 2.9 fusion.169
  423.7 8.9 %reduce-scatter.40.cloned.1.call-done = bf16[128,768]{1,0:T(8,128)(2,1)} async-done(((bf16[512,768]{1,0:T(8,128)(2,1)}), bf16[128,768]{1,0:T(8,128)(2,1)}) %reduce-scatter.40.cloned.1.call-update) | async-done | bytes 196624
  432.6 3.4 add_convert_fusion.3
  436.0 22.4 %reduce-scatter.34.cloned.1.call-done = bf16[128,768]{1,0:T(8,128)(2,1)} async-done(((bf16[512,768]{1,0:T(8,128)(2,1)}), bf16[128,768]{1,0:T(8,128)(2,1)}) %reduce-scatter.34.cloned.1.call-update) | async-done | bytes 196624
  461.3 23.5 %reduce-scatter.38.cloned.1.call-done = bf16[128,768]{1,0:T(8,128)(2,1)} async-done(((bf16[512,768]{1,0:T(8,128)(2,1)}), bf16[128,768]{1,0:T(8,128)(2,1)}) %reduce-scatter.38.cloned.1.call-update) | async-done | bytes 196624
  484.8 3.4 add_convert_fusion.4
  492.8 11.4 %fusion.73 = f32[2,3072,768]{2,1,0:T(8,128)} fusion(bf16[144,2,768]{2,1,0:T(2,128)(2,1)} %bitcast.368, f32[144,2,3072]{2,0,1:T(8,128)} %convolution_bitcast_fusion.3), kind=kOutput, calls=%fused_computation.171 | convolution fusion | flops 1366917120 | bytes 22855680 | tf_op jit(solution)/shard_map/ref,red->efd/dot_general | solution.py:289
  504.3 8.8 %reduce-scatter.28.cloned.1.call-done = bf16[192,768]{1,0:T(8,128)(2,1)} async-done(((bf16[768,768]{1,0:T(8,128)(2,1)}), bf16[192,768]{1,0:T(8,128)(2,1)}) %reduce-scatter.28.cloned.1.call-update) | async-done | bytes 294928 | tf_op jit(solution)/shard_map/reduce_scatter | solution.py:392
  513.1 28.3 %reduce-scatter.22.cloned.1.call-done = bf16[192,768]{1,0:T(8,128)(2,1)} async-done(((bf16[768,768]{1,0:T(8,128)(2,1)}), bf16[192,768]{1,0:T(8,128)(2,1)}) %reduce-scatter.22.cloned.1.call-update) | async-done | bytes 294928 | tf_op jit(solution)/shard_map/reduce_scatter | solution.py:383
  541.4 28.3 %reduce-scatter.26.cloned.1.call-done = bf16[192,768]{1,0:T(8,128)(2,1)} async-done(((bf16[768,768]{1,0:T(8,128)(2,1)}), bf16[192,768]{1,0:T(8,128)(2,1)}) %reduce-scatter.26.cloned.1.call-update) | async-done | bytes 294928 | tf_op jit(solution)/shard_map/reduce_scatter | solution.py:389
  569.8 28.3 %reduce-scatter.24.cloned.1.call-done = bf16[192,768]{1,0:T(8,128)(2,1)} async-done(((bf16[768,768]{1,0:T(8,128)(2,1)}), bf16[192,768]{1,0:T(8,128)(2,1)}) %reduce-scatter.24.cloned.1.call-update) | async-done | bytes 294928 | tf_op jit(solution)/shard_map/reduce_scatter | solution.py:386
  598.2 14.0 %add_convert_fusion = bf16[2,3072,768]{2,1,0:T(8,128)(2,1)} fusion(f32[2,3072,768]{2,1,0:T(8,128)} %fusion.73, bf16[144,2,768]{2,1,0:T(2,128)(2,1)} %bitcast.370, f32[144,2,3072]{2,0,1:T(8,128)} %copy-done.9), kind=kOutput, calls=%fused_computation.15 | convolution fusion | flops 1376354304 | bytes 32292864 | tf_op jit(solution)/shard_map/ref,red->efd/dot_general | solution.py:289
  612.3 10.8 %fusion.78 = f32[2,768,3072]{2,1,0:T(8,128)} fusion(bf16[144,2,3072]{2,0,1:T(8,128)(2,1)} %copy-done.19, bf16[144,2,768]{2,1,0:T(2,128)(2,1)} %bitcast.346), kind=kOutput, calls=%fused_computation.176 | convolution fusion | flops 1358954496 | bytes 21086208 | tf_op jit(solution)/shard_map/red,ref->edf/dot_general | solution.py:294
  623.1 11.5 %add_convert_fusion.1 = bf16[2,768,3072]{2,1,0:T(8,128)(2,1)} fusion(f32[2,768,3072]{2,1,0:T(8,128)} %fusion.78, bf16[144,2,3072]{2,0,1:T(8,128)(2,1)} %copy-done.25, bf16[144,2,768]{2,1,0:T(2,128)(2,1)S(1)} %bitcast.348), kind=kOutput, calls=%fused_computation.16 | convolution fusion | flops 1368391680 | bytes 30523392 | tf_op jit(solution)/shard_map/red,ref->edf/dot_general | solution.py:294
  635.9 5.1 copy.225
  641.0 3.5 copy.224
  644.5 6.2 fusion.29
  650.8 4.7 fusion.32
  668.3 6.0 all-reduce.12
  674.5 22.7 %all-reduce.10 = (bf16[192,16]{0,1:T(8,128)(2,1)S(1)}, bf16[192]{0:T(256)(128)(2,1)S(1)}, bf16[192]{0:T(256)(128)(2,1)S(1)}, bf16[96]{0:T(256)(128)(2,1)S(1)}) all-reduce(bf16[192,16]{0,1:T(8,128)(2,1)} %copy.261, bf16[192]{0:T(256)(128)(2,1)S(1)} %dynamic-slice.10, ...), channel_id=1, replica_groups=mesh['expert'=8,'shard'=4] {'expert'}, use_global_device_ids=true, to_apply=%region_53.54 | all-reduce | flops 3552 | bytes 14208 | tf_op jit(solution)/shard_map/psum | solution.py:413
  701.4 4.3 all-reduce.16.cloned.1.call-done
  713.0 73.0 %reduce-scatter.32.cloned.1.call-done = bf16[2,768,768]{2,1,0:T(8,128)(2,1)} async-done(((bf16[2,3072,768]{2,1,0:T(8,128)(2,1)}), bf16[2,768,768]{2,1,0:T(8,128)(2,1)}) %reduce-scatter.32.cloned.1.call-update) | async-done | bytes 2359312 | tf_op jit(solution)/shard_map/reduce_scatter | solution.py:422
  786.0 4.2 convert_element_type.620
  790.2 76.9 %reduce-scatter.30.cloned.1.call-done = bf16[2,768,768]{2,1,0:T(8,128)(2,1)} async-done(((bf16[2,768,3072]{2,1,0:T(8,128)(2,1)}), bf16[2,768,768]{2,1,0:T(8,128)(2,1)}) %reduce-scatter.30.cloned.1.call-update) | async-done | bytes 2359312 | tf_op jit(solution)/shard_map/reduce_scatter | solution.py:419
  867.1 4.2 convert_element_type.618
  (501 shorter events, 174.6 us)
Async XLA Ops:
  7.2 87.7 %all-gather.10.cloned.1.call-start = ((), (), s32[]{:S(2)}) async-start(), calls=%async_computation.20 | async-start | bytes 1474560 | tf_op jit(solution)/shard_map/all_gather | solution.py:96
  7.9 92.2 %all-gather.8.cloned.1.call-start = ((), (), s32[]{:S(2)}) async-start(), calls=%async_computation.19 | async-start | bytes 1474560 | tf_op jit(solution)/shard_map/all_gather | solution.py:98
  8.7 107.8 %all-gather.12.cloned.1.call-start = ((), (), s32[]{:S(2)}) async-start(), calls=%async_computation.21 | async-start | bytes 1474560 | tf_op jit(solution)/shard_map/all_gather | solution.py:97
  9.4 158.0 %all-gather.14.cloned.1.call-start = ((), (), s32[]{:S(2)}) async-start(), calls=%async_computation.22 | async-start | bytes 1474560 | tf_op jit(solution)/shard_map/all_gather | solution.py:99
  10.0 191.3 %all-gather.16.cloned.1.call-start = ((), (), s32[]{:S(2)}) async-start(), calls=%async_computation.23 | async-start | bytes 11796480 | tf_op jit(solution)/shard_map/all_gather | solution.py:112
  10.6 24.1 %copy-start.105 = (u32[32]{0:T(128)S(1)}, u32[32]{0:T(128)}, u32[]{:S(2)}) copy-start(u32[32]{0:T(128)} %constant.309) | copy-start | bytes 388
  10.6 26.0 %copy-start.109 = (bf16[192]{0:T(256)(128)(2,1)S(1)}, bf16[192]{0:T(256)(128)(2,1)}, u32[]{:S(2)}) copy-start(bf16[192]{0:T(256)(128)(2,1)} %param.23) | copy-start | bytes 1156
  10.6 26.2 %copy-start.110 = (bf16[192]{0:T(256)(128)(2,1)S(1)}, bf16[192]{0:T(256)(128)(2,1)}, u32[]{:S(2)}) copy-start(bf16[192]{0:T(256)(128)(2,1)} %param.24) | copy-start | bytes 1156
  10.6 26.5 %copy-start.111 = (bf16[96]{0:T(256)(128)(2,1)S(1)}, bf16[96]{0:T(256)(128)(2,1)}, u32[]{:S(2)}) copy-start(bf16[96]{0:T(256)(128)(2,1)} %param.25) | copy-start | bytes 580
  10.6 224.9 %all-gather.18.cloned.1.call-start = ((), (), s32[]{:S(2)}) async-start(), calls=%async_computation.24 | async-start | bytes 11796480 | tf_op jit(solution)/shard_map/all_gather | solution.py:113
  30.0 26.6 %copy-start.92 = (bf16[192,16]{0,1:T(8,128)(2,1)S(1)}, bf16[192,16]{0,1:T(8,128)(2,1)}, u32[]{:S(2)}) copy-start(bf16[192,16]{0,1:T(8,128)(2,1)} %param.22) | copy-start | bytes 18436
  33.6 32.0 %copy-start.56 = (bf16[2,128,768]{2,1,0:T(8,128)(2,1)S(1)}, bf16[2,128,768]{2,1,0:T(8,128)(2,1)}, u32[]{:S(2)}) copy-start(bf16[2,128,768]{2,1,0:T(8,128)(2,1)} %param.15) | copy-start | bytes 1179652
  65.0 13.3 %copy-start.41 = (s32[128,512]{0,1:T(8,128)}, s32[128,512]{0,1:T(8,128)S(1)}, u32[]{:S(2)}) copy-start(s32[128,512]{0,1:T(8,128)S(1)} %copy.188) | copy-start | bytes 786436
  81.6 11.1 %copy-start.8 = (bf16[2,128,768]{2,1,0:T(8,128)(2,1)S(1)}, bf16[2,128,768]{2,1,0:T(8,128)(2,1)}, u32[]{:S(2)}) copy-start(bf16[2,128,768]{2,1,0:T(8,128)(2,1)} %param.14) | copy-start | bytes 1179652
  93.4 53.6 %copy-start.75 = (f32[128]{0:T(128)}, f32[128]{0:T(128)S(1)}, u32[]{:S(2)}) copy-start(f32[128]{0:T(128)S(1)} %fusion.161) | copy-start | bytes 1540
  93.4 39.6 %copy-start.77 = (f32[128]{0:T(128)}, f32[128]{0:T(128)S(1)}, u32[]{:S(2)}) copy-start(f32[128]{0:T(128)S(1)} %fusion.163) | copy-start | bytes 1540
  101.9 31.1 %copy-start.10 = (bf16[768,768]{1,0:T(8,128)(2,1)S(1)}, bf16[768,768]{1,0:T(8,128)(2,1)}, u32[]{:S(2)}) copy-start(bf16[768,768]{1,0:T(8,128)(2,1)} %all-gather.8.cloned.1.call-done) | copy-start | bytes 3538948
  118.2 28.8 %copy-start.13 = (bf16[768,768]{1,0:T(8,128)(2,1)S(1)}, bf16[768,768]{1,0:T(8,128)(2,1)}, u32[]{:S(2)}) copy-start(bf16[768,768]{1,0:T(8,128)(2,1)} %all-gather.12.cloned.1.call-done) | copy-start | bytes 3538948
  147.0 40.9 %copy-start.20 = (bf16[512,768]{0,1:T(8,128)(2,1)}, bf16[512,768]{0,1:T(8,128)(2,1)S(1)}, u32[]{:S(2)}) copy-start(bf16[512,768]{0,1:T(8,128)(2,1)S(1)} %copy.199) | copy-start | bytes 2359300
  174.9 8.9 %copy-start.22 = (bf16[512,768]{0,1:T(8,128)(2,1)S(1)}, bf16[512,768]{0,1:T(8,128)(2,1)}, u32[]{:S(2)}) copy-start(bf16[512,768]{0,1:T(8,128)(2,1)} %copy.201) | copy-start | bytes 2359300
  174.9 8.9 %copy-start.53 = (bf16[128,768]{0,1:T(8,128)(2,1)S(1)}, bf16[128,768]{0,1:T(8,128)(2,1)}, u32[]{:S(2)}) copy-start(bf16[128,768]{0,1:T(8,128)(2,1)} %copy.200) | copy-start | bytes 589828
  174.9 9.0 %copy-start.65 = (pred[128,512]{1,0:T(8,128)(4,1)S(1)}, pred[128,512]{1,0:T(8,128)(4,1)}, u32[]{:S(2)}) copy-start(pred[128,512]{1,0:T(8,128)(4,1)} %fusion.112) | copy-start | bytes 196612
  178.0 19.2 %all-to-all-start = ((bf16[8,18,2,768]{3,2,1,0:T(2,128)(2,1)}), bf16[8,18,2,768]{3,2,1,0:T(2,128)(2,1)S(1)}, u32[]{:S(2)}, u32[]{:S(2)}) async-start(bf16[8,18,2,768]{3,2,1,0:T(2,128)(2,1)} %reshape.922), calls=%async_computation | async-start | bytes 884736 | tf_op jit(solution)/shard_map/all_to_all | solution.py:245
  191.3 77.1 %copy-start.108 = (f32[128]{0:T(128)}, f32[128]{0:T(128)S(1)}, u32[]{:S(2)}) copy-start(f32[128]{0:T(128)S(1)} %get-tuple-element.293) | copy-start | bytes 1540
  197.2 11.2 %copy-start.16 = (bf16[8,18,2,768]{3,2,1,0:T(2,128)(2,1)}, bf16[8,18,2,768]{3,2,1,0:T(2,128)(2,1)S(1)}, u32[]{:S(2)}) copy-start(bf16[8,18,2,768]{3,2,1,0:T(2,128)(2,1)S(1)} %all-to-all-done) | copy-start | bytes 1327108
  197.2 46.1 %all-to-all-start.4 = ((bf16[8,18,2,768]{3,2,1,0:T(2,128)(2,1)}), bf16[8,18,2,768]{3,2,1,0:T(2,128)(2,1)S(1)}, u32[]{:S(2)}, u32[]{:S(2)}) async-start(bf16[8,18,2,768]{3,2,1,0:T(2,128)(2,1)} %convert_element_type.554), calls=%async_computation.4 | async-start | bytes 884736 | tf_op jit(solution)/shard_map/all_to_all | solution.py:283
  242.2 15.5 %slice-start = ((s8[9437184]{0:T(1024)(128)(4,1)}), s8[1048576]{0:T(1024)(128)(4,1)S(1)}, s32[]{:S(2)}) async-start(s8[9437184]{0:T(1024)(128)(4,1)} %bitcast.343), calls=%async_computation.37 | async-start | bytes 2097152
  243.3 18.8 %all-to-all-start.1 = ((bf16[8,18,2,768]{3,2,1,0:T(2,128)(2,1)}), bf16[8,18,2,768]{3,2,1,0:T(2,128)(2,1)}, u32[]{:S(2)}, u32[]{:S(2)}) async-start(bf16[8,18,2,768]{3,2,1,0:T(2,128)(2,1)} %bitcast.34), calls=%async_computation.1 | async-start | bytes 884736 | tf_op jit(solution)/shard_map/all_to_all | solution.py:258
  248.9 8.9 %slice-start.1 = ((s8[9437184]{0:T(1024)(128)(4,1)}), s8[4194304]{0:T(1024)(128)(4,1)S(1)}, s32[]{:S(2)}) async-start(s8[9437184]{0:T(1024)(128)(4,1)} %bitcast.343), calls=%async_computation.38 | async-start | bytes 8388608
  248.9 8.9 %slice-start.2 = ((s8[9437184]{0:T(1024)(128)(4,1)}), s8[4194304]{0:T(1024)(128)(4,1)S(1)}, s32[]{:S(2)}) async-start(s8[9437184]{0:T(1024)(128)(4,1)} %bitcast.343), calls=%async_computation.39 | async-start | bytes 8388608
  257.7 11.9 %copy-start.91 = (s32[1024]{0:T(1024)S(1)}, s32[1024]{0:T(1024)}, u32[]{:S(2)}) copy-start(s32[1024]{0:T(1024)} %pad_clamp_fusion.4) | copy-start | bytes 12292
  262.1 9.2 %copy-start.36 = (f32[128,768]{1,0:T(8,128)S(1)}, f32[128,768]{1,0:T(8,128)}, u32[]{:S(2)}) copy-start(f32[128,768]{1,0:T(8,128)} %copy-done.35) | copy-start | bytes 1179652
  262.1 9.2 %copy-start.64 = (f32[128,2]{1,0:T(8,128)S(1)}, f32[128,2]{1,0:T(8,128)}, u32[]{:S(2)}) copy-start(f32[128,2]{1,0:T(8,128)} %copy-done.63) | copy-start | bytes 3076
  262.1 18.9 %all-to-all-start.5 = ((bf16[8,18,2,768]{3,2,1,0:T(2,128)(2,1)}), bf16[8,18,2,768]{3,2,1,0:T(2,128)(2,1)S(1)}, u32[]{:S(2)}, u32[]{:S(2)}) async-start(bf16[8,18,2,768]{3,2,1,0:T(2,128)(2,1)} %bitcast.69), calls=%async_computation.5 | async-start | bytes 884736 | tf_op jit(solution)/shard_map/all_to_all | solution.py:303
  268.4 101.5 %copy-start.97 = (f32[128]{0:T(128)}, f32[128]{0:T(128)S(1)}, u32[]{:S(2)}) copy-start(f32[128]{0:T(128)S(1)} %fusion.164) | copy-start | bytes 1540
  273.5 10.2 %copy-start.68 = (bf16[128,16]{0,1:T(8,128)(2,1)}, bf16[128,16]{0,1:T(8,128)(2,1)S(1)}, u32[]{:S(2)}) copy-start(bf16[128,16]{0,1:T(8,128)(2,1)S(1)} %select_reduce_fusion.1) | copy-start | bytes 12292
  288.5 16.2 %all-to-all-start.2 = ((bf16[8,18,2,768]{3,2,1,0:T(2,128)(2,1)}), bf16[8,18,2,768]{3,2,1,0:T(2,128)(2,1)S(1)}, u32[]{:S(2)}, u32[]{:S(2)}) async-start(bf16[8,18,2,768]{3,2,1,0:T(2,128)(2,1)} %reshape.930), calls=%async_computation.2 | async-start | bytes 884736 | tf_op jit(solution)/shard_map/all_to_all | solution.py:245
  304.7 8.9 %copy-start.17 = (bf16[8,18,2,768]{3,2,1,0:T(2,128)(2,1)}, bf16[8,18,2,768]{3,2,1,0:T(2,128)(2,1)S(1)}, u32[]{:S(2)}) copy-start(bf16[8,18,2,768]{3,2,1,0:T(2,128)(2,1)S(1)} %all-to-all-done.2) | copy-start | bytes 1327108
  304.7 17.0 %all-to-all-start.6 = ((bf16[8,18,2,768]{3,2,1,0:T(2,128)(2,1)}), bf16[8,18,2,768]{3,2,1,0:T(2,128)(2,1)S(1)}, u32[]{:S(2)}, u32[]{:S(2)}) async-start(bf16[8,18,2,768]{3,2,1,0:T(2,128)(2,1)} %convert_element_type.576), calls=%async_computation.6 | async-start | bytes 884736 | tf_op jit(solution)/shard_map/all_to_all | solution.py:283
  321.7 16.6 %copy-start.45 = (bf16[8,18,2,768]{3,2,1,0:T(2,128)(2,1)}, bf16[8,18,2,768]{3,2,1,0:T(2,128)(2,1)S(1)}, u32[]{:S(2)}) copy-start(bf16[8,18,2,768]{3,2,1,0:T(2,128)(2,1)S(1)} %all-to-all-done.6) | copy-start | bytes 1327108
  321.7 25.5 %all-to-all-start.3 = ((bf16[8,18,2,768]{3,2,1,0:T(2,128)(2,1)}), bf16[8,18,2,768]{3,2,1,0:T(2,128)(2,1)S(1)}, u32[]{:S(2)}, u32[]{:S(2)}) async-start(bf16[8,18,2,768]{3,2,1,0:T(2,128)(2,1)} %bitcast.63), calls=%async_computation.3 | async-start | bytes 884736 | tf_op jit(solution)/shard_map/all_to_all | solution.py:258
  338.4 7.7 copy-start.25
  338.4 14.9 %copy-start.101 = (s32[256,1]{0,1:T(1,128)S(1)}, s32[256,1]{0,1:T(1,128)}, u32[]{:S(2)}) copy-start(s32[256,1]{0,1:T(1,128)} %copy-done.100) | copy-start | bytes 3076
  338.4 14.9 %copy-start.107 = (f32[128]{0:T(128)S(1)}, f32[128]{0:T(128)}, u32[]{:S(2)}) copy-start(f32[128]{0:T(128)} %copy-done.106) | copy-start | bytes 1540
  347.2 17.4 %all-to-all-start.7 = ((bf16[8,18,2,768]{3,2,1,0:T(2,128)(2,1)}), bf16[8,18,2,768]{3,2,1,0:T(2,128)(2,1)S(1)}, u32[]{:S(2)}, u32[]{:S(2)}) async-start(bf16[8,18,2,768]{3,2,1,0:T(2,128)(2,1)} %bitcast.85), calls=%async_computation.7 | async-start | bytes 884736 | tf_op jit(solution)/shard_map/all_to_all | solution.py:303
  353.2 67.6 %reduce-scatter.36.cloned.1.call-start = ((), (), s32[]{:S(2)}) async-start(), calls=%async_computation.32 | async-start | bytes 983040
  371.4 8.7 copy-start.1
  385.0 47.6 %reduce-scatter.40.cloned.1.call-start = ((), (), s32[]{:S(2)}) async-start(), calls=%async_computation.34 | async-start | bytes 983040
  395.9 62.5 %reduce-scatter.34.cloned.1.call-start = ((), (), s32[]{:S(2)}) async-start(), calls=%async_computation.31 | async-start | bytes 983040
  404.6 80.2 %reduce-scatter.38.cloned.1.call-start = ((), (), s32[]{:S(2)}) async-start(), calls=%async_computation.33 | async-start | bytes 983040
  411.1 102.0 %reduce-scatter.28.cloned.1.call-start = ((), (), s32[]{:S(2)}) async-start(), calls=%async_computation.28 | async-start | bytes 1474560 | tf_op jit(solution)/shard_map/reduce_scatter | solution.py:392
  414.4 127.0 %reduce-scatter.22.cloned.1.call-start = ((), (), s32[]{:S(2)}) async-start(), calls=%async_computation.25 | async-start | bytes 1474560 | tf_op jit(solution)/shard_map/reduce_scatter | solution.py:383
  420.7 149.1 %reduce-scatter.26.cloned.1.call-start = ((), (), s32[]{:S(2)}) async-start(), calls=%async_computation.27 | async-start | bytes 1474560 | tf_op jit(solution)/shard_map/reduce_scatter | solution.py:389
  436.0 162.2 %reduce-scatter.24.cloned.1.call-start = ((), (), s32[]{:S(2)}) async-start(), calls=%async_computation.26 | async-start | bytes 1474560 | tf_op jit(solution)/shard_map/reduce_scatter | solution.py:386
  461.3 27.0 %copy-start.69 = (bf16[128,16]{0,1:T(8,128)(2,1)S(1)}, bf16[128,16]{0,1:T(8,128)(2,1)}, u32[]{:S(2)}) copy-start(bf16[128,16]{0,1:T(8,128)(2,1)} %copy-done.68) | copy-start | bytes 12292
  461.3 28.0 %copy-start.71 = (bf16[128,16]{0,1:T(8,128)(2,1)S(1)}, bf16[128,16]{0,1:T(8,128)(2,1)}, u32[]{:S(2)}) copy-start(bf16[128,16]{0,1:T(8,128)(2,1)} %copy-done.70) | copy-start | bytes 12292
  488.2 171.9 %reduce-scatter.42.cloned.1.call-start = ((), (), s32[]{:S(2)}) async-start(), calls=%async_computation.35 | async-start | bytes 245760
  492.6 213.1 %all-reduce.16.cloned.1.call-start = ((), (), s32[]{:S(2)}) async-start(), calls=%async_computation.36 | async-start | bytes 2359296 | tf_op jit(solution)/shard_map/psum | solution.py:409
  598.1 187.8 %reduce-scatter.32.cloned.1.call-start = ((), (), s32[]{:S(2)}) async-start(), calls=%async_computation.30 | async-start | bytes 11796480 | tf_op jit(solution)/shard_map/reduce_scatter | solution.py:422
  612.3 254.8 %reduce-scatter.30.cloned.1.call-start = ((), (), s32[]{:S(2)}) async-start(), calls=%async_computation.29 | async-start | bytes 11796480 | tf_op jit(solution)/shard_map/reduce_scatter | solution.py:419
  612.3 10.8 %copy-start.18 = (bf16[8,18,2,768]{3,2,1,0:T(2,128)(2,1)S(1)}, bf16[8,18,2,768]{3,2,1,0:T(2,128)(2,1)}, u32[]{:S(2)}) copy-start(bf16[8,18,2,768]{3,2,1,0:T(2,128)(2,1)} %copy-done.17) | copy-start | bytes 1327108
  650.8 8.0 copy-start.48
  663.5 36.6 %copy-start.28 = (f32[128,768]{1,0:T(8,128)S(1)}, f32[128,768]{1,0:T(8,128)}, u32[]{:S(2)}) copy-start(f32[128,768]{1,0:T(8,128)} %copy-done.26) | copy-start | bytes 1179652
  663.6 36.6 %copy-start.29 = (f32[128,768]{1,0:T(8,128)S(1)}, f32[128,768]{1,0:T(8,128)}, u32[]{:S(2)}) copy-start(f32[128,768]{1,0:T(8,128)} %get-tuple-element.219) | copy-start | bytes 1179652
  (79 other events, 298.3 us)
Sparse Core Ops, SparseCore 0:
  9.6 20.1 all-gather.9
  31.3 17.7 all-gather.7
  50.7 17.5 all-gather.11
  69.7 17.5 all-gather.13
  88.7 81.0 all-gather.15
  171.2 64.2 all-gather.17
  385.1 21.4 reduce-scatter.35
  409.3 23.2 reduce-scatter.39
  435.1 23.2 reduce-scatter.33
  461.5 23.2 reduce-scatter.37
  487.3 25.7 reduce-scatter.27
  515.7 25.7 reduce-scatter.21
  544.0 25.7 reduce-scatter.25
  572.4 25.7 reduce-scatter.23
  601.0 19.7 reduce-scatter.41
  624.5 81.1 all-reduce.15
  708.3 77.6 reduce-scatter.31
  788.6 78.4 reduce-scatter.29
where the time goes:
time: 885 us; the launch traced here: 878 us
  waiting for transfers between devices  366 us (41%)
  matrix products  194 us (22%)
  local copies, waits for them, and re-layouts  105 us (12%)
  blocking collectives  96.7 us (11%)
  other arithmetic  56 us (6%)
  starting transfers between devices  42.5 us (5%)
  between operations  19.1 us (2%)
    reduce_scatter x1, waiting for transfers between devices, per_device(): lax.psum_scatter(sum_expert_in.astype(jnp.bfloat16), 'shard', scatter_dim...  76.9 us
    reduce_scatter x1, waiting for transfers between devices, per_device(): lax.psum_scatter(sum_expert_out.astype(jnp.bfloat16), 'shard', scatter_di...  73 us
    unnamed x23, waiting for transfers between devices  58.6 us
    reduce_scatter x1, waiting for transfers between devices, per_device(): lax.psum_scatter(sum_value.astype(jnp.bfloat16), 'shard', scatter_dimensi...  28.3 us
    reduce_scatter x1, waiting for transfers between devices, per_device(): lax.psum_scatter(sum_query.astype(jnp.bfloat16), 'shard', scatter_dimensi...  28.3 us
    reduce_scatter x1, waiting for transfers between devices, per_device(): lax.psum_scatter(sum_key.astype(jnp.bfloat16), 'shard', scatter_dimension...  28.3 us
    all_gather x1, waiting for transfers between devices, per_device(): lax.all_gather(w_out, 'shard', axis=1, tiled=True)  27.1 us
    all_gather x2, blocking collectives, per_device(): lax.all_gather(key, 'shard', axis=0, tiled=True)  27 us
  transfers between devices with their start and end apart: 26, of which 15 were waited for; matrix products, arithmetic and copies ran while one was open for 36% of the time, Pallas kernels for 0%

commit v1 on v0

--- a/solution.py
+++ b/solution.py
@@ -1,18 +1,1327 @@
+import functools
 from functools import reduce
 import math
 
 import jax
 import jax.numpy as jnp
+import numpy as np
 from jax import lax
+from jax.experimental import pallas as pl
+from jax.experimental.pallas import tpu as pltpu
 from jax.sharding import PartitionSpec as P
 
 HEADS = 12
 BUCKETS = 32
-
-
 EPS = 1e-06
 MASKED = -1e30
 BUCKET_EDGES = (24, 32, 48, 64, 96, 128, 192, 256, 384, 512, 768, 1024, 1536, 2048, 3072)
+MESH = pl.DeviceIdType.MESH
+BF = jnp.bfloat16
+F32 = jnp.float32
+I32 = jnp.int32
+LANES = 128
+
+
+class Sizes:
+    def __init__(self, ne, ns, micro, rows, width, experts, local_experts, ff):
+        self.ne, self.ns, self.ny = ne, ns, ns // 2
+        self.m, self.t, self.d = micro, rows, width
+        self.e, self.el, self.ff = experts, local_experts, ff
+        self.g = ns * rows
+        self.mt = micro * rows
+        self.r = width // ns
+        self.cap = (9 * rows + 4 * experts - 1) // (4 * experts)
+        self.per = micro * self.cap
+        self.sp = -(-(local_experts * self.per + 2) // 16) * 16
+        self.slots = ne * self.sp
+        self.nz = ne // 2
+        self.hn = ne // 2
+        self.cr = self.hn * self.per
+        self.cb = local_experts * self.cr
+        self.blk = 2 * self.cb
+        self.hs = self.hn * self.sp
+        self.n16 = -(-ne // 16) * 16
+        self.pairs = HEADS // 2
+        self.small = experts + 16
+        self.far = self.g // 2 + rows
+
+    def fits(self):
+        return (
+            self.ns % 2 == 0
+            and self.t == LANES
+            and self.d == HEADS * 64
+            and self.cr % 16 == 0
+            and self.ne % 4 == 0
+            and self.e % 16 == 0
+            and self.r % (16 * self.nz) == 0
+            and self.slots % LANES == 0
+            and self.el * self.per <= LANES
+            and self.d % 256 == 0
+        )
+
+
+def layout_constants(z):
+    perm = np.zeros((z.cb, z.hs), np.float32)
+    rows_of = np.zeros((2 * z.n16, z.slots), np.float32)
+    dest = np.zeros((2 * z.n16, z.slots), np.float32)
+    place = np.zeros((z.slots, LANES), np.float32)
+    gate_of = np.zeros((2 * z.n16, z.hs), np.float32)
+    source = np.zeros((z.cb, 2 * z.n16), np.float32)
+    pick = np.zeros((z.cb, LANES), np.float32)
+    used = z.el * z.per
+    for src in range(z.ne):
+        rows_of[src, src * z.sp + used] = 1
+        rows_of[z.n16 + src, src * z.sp + used + 1] = 1
+        dest[src, src * z.sp : (src + 1) * z.sp] = 1
+        dest[z.n16 + src, src * z.sp : (src + 1) * z.sp] = 1
+        for q in range(used):
+            place[src * z.sp + q, q] = 1
+    for src in range(z.hn):
+        gate_of[src, src * z.sp + used] = 1
+        gate_of[z.n16 + src, src * z.sp + used + 1] = 1
+        for q in range(used):
+            row = (q // z.per) * z.cr + src * z.per + q % z.per
+            perm[row, src * z.sp + q] = 1
+            source[row, src] = 1
+            source[row, z.n16 + src] = 1
+            pick[row, q] = 1
+    return [jnp.asarray(a, BF) for a in (perm, rows_of, dest, place, gate_of, source, pick)]
+
+
+def dot(a, b):
+    return jnp.dot(a, b, preferred_element_type=F32)
+
+
+def dot_t(a, b):
+    return lax.dot_general(a, b, (((1,), (1,)), ((), ())), preferred_element_type=F32)
+
+
+def tdot(a, b):
+    return lax.dot_general(a, b, (((0,), (0,)), ((), ())), preferred_element_type=F32)
+
+
+def iota(shape, dim):
+    return lax.broadcasted_iota(I32, shape, dim)
+
+
+def aligned(start, size, multiple):
+    return pl.ds(pl.multiple_of(start, multiple), size)
+
+
+def offsets(z, chunk=None):
+    every = [(kz, kx) for kz in range(z.nz) for kx in range(2)][1:]
+    return [k for k in every if chunk is None or k[0] % 2 == chunk]
+
+
+def position(z, k):
+    return (k[0] % 2) * z.hn + (k[0] // 2) * 2 + k[1]
+
+
+class Place:
+    def __init__(self, z):
+        self.z = z
+        self.e = lax.axis_index("expert")
+        self.s = lax.axis_index("shard")
+        self.y, self.c = lax.div(self.s, 2), lax.rem(self.s, 2)
+
+    def shard(self, k, other):
+        y = lax.rem(self.y + k, self.z.ny)
+        return y * 2 + (1 - self.c if other else self.c)
+
+    def expert(self, kz, kx):
+        high = lax.rem(lax.div(self.e, 2) + kz, self.z.nz)
+        return high * 2 + lax.rem(lax.rem(self.e, 2) + kx, 2)
+
+    def barrier(self, with_experts=True):
+        sem = pltpu.get_barrier_semaphore()
+        others = [(self.e, self.shard(0, True))]
+        others += [(self.e, self.shard(k, False)) for k in range(1, self.z.ny)]
+        if with_experts:
+            others += [(self.expert(*k), self.s) for k in offsets(self.z)]
+        for other in others:
+            pl.semaphore_signal(sem, inc=1, device_id=other, device_id_type=MESH)
+        pl.semaphore_wait(sem, len(others))
+
+
+def rcopy(src, dst, send, recv, to):
+    return pltpu.make_async_remote_copy(
+        src_ref=src, dst_ref=dst, send_sem=send, recv_sem=recv, device_id=to, device_id_type=MESH
+    )
+
+
+class Gather:
+    def __init__(self, place, own, full, send, recv, item):
+        self.p, self.own, self.full = place, own, full
+        self.send, self.recv, self.item = send, recv, item
+
+    def copy(self, origin, src, slot, to):
+        return rcopy(
+            src, self.full(origin), self.send.at[self.item, slot], self.recv.at[self.item, origin], to
+        )
+
+    def partner(self):
+        return (self.p.e, self.p.shard(0, True))
+
+    def start(self):
+        p, ny = self.p, self.p.z.ny
+        for k in range(1, ny):
+            self.copy(p.s, self.own, k, (p.e, p.shard(k, False))).start()
+        self.copy(p.s, self.own, 0, self.partner()).start()
+
+    def forward(self):
+        p, ny = self.p, self.p.z.ny
+        for k in range(1, ny):
+            origin = p.shard(k, False)
+            self.copy(origin, self.full(origin), ny + k - 1, self.partner()).wait_recv()
+            self.copy(origin, self.full(origin), ny + k - 1, self.partner()).start()
+
+    def arrive(self):
+        p, ny = self.p, self.p.z.ny
+        for k in range(ny):
+            origin = p.shard(k, True)
+            self.copy(origin, self.full(origin), 0, self.partner()).wait_recv()
+
+    def finish(self):
+        p, ny = self.p, self.p.z.ny
+        for slot in range(2 * ny - 1):
+            self.copy(p.s, self.own, slot, self.partner()).wait_send()
+
+
+class Exchange:
+    def __init__(self, place, src, dst, send, recv, item):
+        self.p, self.src, self.dst = place, src, dst
+        self.send, self.recv, self.item = send, recv, item
+
+    def copy(self, k):
+        z = self.p.z
+        back = (-k[0] % z.nz, k[1])
+        at = position(z, back)
+        to = self.p.expert(*k)
+        return rcopy(
+            self.src(to),
+            self.dst(at),
+            self.send.at[self.item, position(z, k)],
+            self.recv.at[self.item, at],
+            (to, self.p.s),
+        )
+
+    def start(self, chunk=None):
+        for k in offsets(self.p.z, chunk):
+            self.copy(k).start()
+
+    def arrive(self, chunk=None):
+        z = self.p.z
+        for k in offsets(z, chunk):
+            self.copy((-k[0] % z.nz, k[1])).wait_recv()
+
+    def finish(self):
+        for k in offsets(self.p.z):
+            self.copy(k).wait_send()
+
+
+def slot_ids(z, routes):
+    lane = iota((z.t, LANES), 1)
+    lower = (iota((z.t, z.t), 0) > iota((z.t, z.t), 1)).astype(F32).astype(BF)
+    base = lane * z.per
+    for d in range(1, z.ne):
+        base = base + jnp.where(lane >= d * z.el, z.sp - z.el * z.per, 0)
+    firsts, seconds = [], []
+    for m in range(z.m):
+        r0 = routes[m * z.t : (m + 1) * z.t, 0:1]
+        r1 = routes[m * z.t : (m + 1) * z.t, 1:2]
+        hit0, hit1 = lane == r0, lane == r1
+        hits = jnp.where(hit0 | hit1, 1.0, 0.0).astype(BF)
+        spot = dot(lower, hits) + (base + m * z.cap).astype(F32)
+        firsts.append(jnp.sum(jnp.where(hit0, spot, 0.0), axis=1, keepdims=True))
+        seconds.append(jnp.sum(jnp.where(hit1, spot, 0.0), axis=1, keepdims=True))
+    return jnp.concatenate(firsts, 0), jnp.concatenate(seconds, 0)
+
+
+def one_hot(z, slot):
+    return (iota((z.mt, z.slots), 1) == slot.astype(I32)).astype(F32)
+
+
+def key_layout(z, counts, m, shape, dim):
+    row = iota(shape, dim)
+    total = counts[m, 0]
+    for b in range(1, z.ns):
+        total = total + counts[m, b]
+    position = jnp.zeros(shape, I32)
+    prompt = jnp.zeros(shape, I32)
+    offset = 0
+    for b in range(z.ns):
+        own = counts[m, b]
+        local = row - b * z.t
+        inside = (local >= 0) & (local < z.t)
+        first = local < own
+        position = jnp.where(inside, jnp.where(first, offset + local, total + local - own), position)
+        prompt = jnp.where(inside & first, 1, prompt)
+        offset = offset + own
+    return position, prompt
+
+
+def query_position(z, counts, m, s):
+    total, offset, own = 0, 0, 0
+    for b in range(z.ns):
+        count = counts[m, b]
+        total = total + count
+        offset = offset + jnp.where(b < s, count, 0)
+        own = own + jnp.where(b == s, count, 0)
+    local = iota((z.t, 1), 0)
+    return jnp.where(local < own, offset + local, total + local - own)
+
+
+def bucket_of(z, distance):
+    coarse = jnp.full(distance.shape, 16, I32)
+    for edge in BUCKET_EDGES:
+        if edge < z.far:
+            coarse = coarse + jnp.where(distance >= edge, 1, 0)
+    return jnp.where(distance < 16, distance, coarse)
+
+
+def front_kernel(
+    z,
+    tokens, dy, routes, counts, wk, wv, wq, wo, small, perm, rows_of, dest, place_m,
+    toks, hid, kk, vv, qq, pp, ctx, mid, nrm, sd, xs, dyg, fk, fv, fq, fo, smallg,
+    dys, dyr, table, bias_id, bias_mask,
+    gsend, grecv, xsend, xrecv,
+):
+    p = Place(z)
+    p.barrier()
+    mt, t, d, r = z.mt, z.t, z.d, z.r
+
+    def rows(ref, size):
+        return lambda origin: ref.at[aligned(origin * size, size, 16)]
+
+    items = [Gather(p, small, lambda o: smallg.at[o], gsend, grecv, 0)]
+    for m in range(z.m):
+        items.append(
+            Gather(
+                p,
+                tokens.at[m],
+                lambda o, m=m: toks.at[m, aligned(o * t, t, 16)],
+                gsend,
+                grecv,
+                1 + m,
+            )
+        )
+    base = 1 + z.m
+    for i, (own, full) in enumerate(((wk, fk), (wv, fv), (wq, fq), (wo, fo))):
+        items.append(Gather(p, own, rows(full, r), gsend, grecv, base + i))
+    for item in items:
+        item.start()
+    g_dy = Gather(p, dyg.at[p.s], lambda o: dyg.at[o], gsend, grecv, base + 4)
+    x_dy = Exchange(
+        p,
+        lambda to: dys.at[aligned(to * z.sp, z.sp, 16)],
+        lambda at: dyr.at[pl.ds(at * z.sp, z.sp)],
+        xsend,
+        xrecv,
+        0,
+    )
+    smallg[p.s] = small[...]
+    for m in range(z.m):
+        toks[m, aligned(p.s * t, t, 16), :] = tokens[m]
+    for own, full in ((wk, fk), (wv, fv), (wq, fq), (wo, fo)):
+        full[aligned(p.s * r, r, 16), :] = own[...]
+
+    slot0, slot1 = slot_ids(z, routes)
+    hot = (one_hot(z, slot0) + one_hot(z, slot1)).astype(BF)
+
+    def send_dy(i, carry):
+        cols = aligned(i * 256, 256, 256)
+        dys[:, cols] = tdot(hot, dy[:, cols]).astype(BF)
+        return carry
+
+    lax.fori_loop(0, d // 256, send_dy, 0)
+    x_dy.start()
+    mine = aligned(p.e * z.sp, z.sp, 16)
+    dyr[0 : z.sp, :] = dys[mine, :]
+
+    for m in range(z.m):
+        key_pos, prompt = key_layout(z, counts, m, (1, z.g), 1)
+        distance = query_position(z, counts, m, p.s) - key_pos
+        lane = iota((1, z.g), 1)
+        own_block = (lane >= p.s * t) & (lane < (p.s + 1) * t)
+        visible = (distance >= 0) & (own_block | (prompt == 1))
+        bias_id[m] = jnp.where(visible, bucket_of(z, distance), 0)
+        bias_mask[m] = jnp.where(visible, 0.0, MASKED)
+
+    for item in items[: 1 + z.m]:
+        item.forward()
+    for item in items[: 1 + z.m]:
+        item.arrive()
+    sums = smallg[0].astype(F32)
+    for b in range(1, z.ns):
+        sums = sums + smallg[b].astype(F32)
+    gain_one = sums[z.e : z.e + 1, :]
+    gain_two = sums[z.e + 1 : z.e + 2, :]
+    router = sums.astype(BF)
+    for i in range(HEADS * BUCKETS // LANES):
+        table[:, i * LANES : (i + 1) * LANES] = jnp.broadcast_to(
+            sums[z.e + 2 : z.e + 3, i * LANES : (i + 1) * LANES], (8, LANES)
+        )
+    for m in range(z.m):
+        def norm(i, carry, m=m):
+            at = aligned(i * t, t, 16)
+            x = toks[m, at, :].astype(F32)
+            scale = lax.rsqrt(jnp.mean(x * x, axis=1, keepdims=True) + EPS)
+            hid[m, at, :] = (x * scale * gain_one).astype(BF)
+            return carry
+
+        lax.fori_loop(0, z.ns, norm, 0)
+
+    for item, full, out in ((items[base], fk, kk), (items[base + 1], fv, vv)):
+        item.forward()
+        item.arrive()
+
+        def project(i, carry, full=full, out=out):
+            m, cols = lax.div(i, d // 256), aligned(lax.rem(i, d // 256) * 256, 256, 256)
+            out[m, :, cols] = dot(hid[m], full[:, cols]).astype(BF)
+            return carry
+
+        lax.fori_loop(0, z.m * (d // 256), project, 0)
+    items[base + 2].forward()
+    items[base + 2].arrive()
+    items[base + 3].forward()
+
+    def project_query(i, carry):
+        m, cols = lax.div(i, d // 256), aligned(lax.rem(i, d // 256) * 256, 256, 256)
+        own = hid[m, aligned(p.s * t, t, 16), :]
+        qq[aligned(m * t, t, 16), cols] = (dot(own, fq[:, cols]).astype(BF).astype(F32) * 0.125).astype(BF)
+        return carry
+
+    lax.fori_loop(0, z.m * (d // 256), project_query, 0)
+
+    x_dy.arrive()
+
+    def order_dy(i, carry):
+        cols = aligned(i * 256, 256, 256)
+        for h in range(2):
+            rows_h = slice(h * z.hs, (h + 1) * z.hs)
+            dyg[p.s, h * z.cb : (h + 1) * z.cb, cols] = dot(perm[...], dyr[rows_h, cols]).astype(BF)
+        return carry
+
+    lax.fori_loop(0, d // 256, order_dy, 0)
+    g_dy.start()
+
+    low = iota((t, LANES), 1) < 64
+
+    def attend(i, carry):
+        m, pair = lax.div(i, z.pairs), lax.rem(i, z.pairs)
+        cols = aligned(pair * LANES, LANES, LANES)
+        q = qq[aligned(m * t, t, 16), cols]
+        zero = jnp.zeros_like(q)
+        q_two = jnp.concatenate([jnp.where(low, q, zero), jnp.where(low, zero, q)], 0)
+        scores = dot_t(q_two, kk[m, :, cols])
+        part = table[0:1, aligned(lax.div(pair, 2) * LANES, LANES, LANES)]
+        part = jnp.broadcast_to(part, (t, LANES))
+        shift = lax.rem(pair, 2) * 64
+        for half in range(2):
+            halves = []
+            for b in range(z.ns):
+                idx = bias_id[m, :, b * LANES : (b + 1) * LANES] + (shift + 32 * half)
+                bias = jnp.take_along_axis(part, idx, axis=1)
+                halves.append(
+                    scores[half * t : (half + 1) * t, b * LANES : (b + 1) * LANES]
+                    + (bias + bias_mask[m, :, b * LANES : (b + 1) * LANES])
+                )
+            s = jnp.concatenate(halves, 1)
+            top = jnp.max(s, axis=1, keepdims=True)
+            e = jnp.exp(s - top)
+            total = jnp.sum(e, axis=1, keepdims=True)
+            pp[i, half * t : (half + 1) * t, :] = (e * (1.0 / total)).astype(BF)
+        two = dot(pp[i], vv[m, :, cols])
+        ctx[aligned(m * t, t, 16), cols] = jnp.where(low, two[:t], two[t:]).astype(BF)
+        return carry
+
+    lax.fori_loop(0, z.m * z.pairs, attend, 0)
+    g_dy.forward()
+    items[base + 3].arrive()
+
+    def output(i, carry):
+        cols = aligned(i * 256, 256, 256)
+        mid[:, cols] = dot(ctx[...], fo[:, cols])
+        return carry
+
+    lax.fori_loop(0, d // 256, output, 0)
+    for m in range(z.m):
+        at = slice(m * t, (m + 1) * t)
+        x = mid[at, :] + tokens[m].astype(F32)
+        mid[at, :] = x
+        scale = lax.rsqrt(jnp.mean(x * x, axis=1, keepdims=True) + EPS)
+        nrm[at, :] = (x * scale * gain_two).astype(BF)
+    logits = dot_t(nrm[...], router)
+    lane = iota((mt, z.small), 1)
+    pick0 = jnp.sum(jnp.where(lane == routes[:, 0:1], logits, 0.0), axis=1, keepdims=True)
+    pick1 = jnp.sum(jnp.where(lane == routes[:, 1:2], logits, 0.0), axis=1, keepdims=True)
+    top = jnp.maximum(pick0, pick1)
+    e0, e1 = jnp.exp(pick0 - top), jnp.exp(pick1 - top)
+    gate0, gate1 = e0 / (e0 + e1), e1 / (e0 + e1)
+    lane = iota((mt, LANES), 1)
+    sd[...] = jnp.where(
+        lane == 0, slot0, jnp.where(lane == 1, slot1, jnp.where(lane == 2, gate0, jnp.where(lane == 3, gate1, 0.0)))
+    )
+    hot0, hot1 = one_hot(z, slot0), one_hot(z, slot1)
+    gate_row = jnp.sum(hot0 * gate0 + hot1 * gate1, axis=0, keepdims=True)
+    high = gate_row.astype(BF).astype(F32)
+    is_high = iota((2 * z.n16, 1), 0) < z.n16
+    gates = (dest[...].astype(F32) * jnp.where(is_high, high, gate_row - high)).astype(BF)
+    gates = dot(gates, place_m[...]).astype(BF)
+    hot = (hot0 + hot1).astype(BF)
+
+    def dispatch(i, carry):
+        cols = aligned(i * 256, 256, 256)
+        xs[:, cols] = tdot(hot, nrm[:, cols]).astype(BF)
+        return carry
+
+    lax.fori_loop(0, d // 256, dispatch, 0)
+    xs[:, :LANES] = (xs[:, :LANES].astype(F32) + tdot(rows_of[...], gates)).astype(BF)
+    g_dy.arrive()
+    for item in items + [g_dy]:
+        item.finish()
+    x_dy.finish()
+
+
+VMEM = pl.BlockSpec(memory_space=pltpu.VMEM)
+SMEM = pl.BlockSpec(memory_space=pltpu.SMEM)
+
+
+def front(z, tokens, dy, routes, counts, wk, wv, wq, wo, small, perm, rows_of, dest, place_m):
+    def bf(*shape):
+        return jax.ShapeDtypeStruct(shape, BF)
+
+    def f32(*shape):
+        return jax.ShapeDtypeStruct(shape, F32)
+
+    outs = (
+        bf(z.m, z.g, z.d), bf(z.m, z.g, z.d), bf(z.m, z.g, z.d), bf(z.m, z.g, z.d), bf(z.mt, z.d),
+        bf(z.m * z.pairs, 2 * z.t, z.g), bf(z.mt, z.d), f32(z.mt, z.d), bf(z.mt, z.d), f32(z.mt, LANES),
+        bf(z.slots, z.d), bf(z.ns, z.blk, z.d), bf(z.d, z.d), bf(z.d, z.d), bf(z.d, z.d), bf(z.d, z.d),
+        bf(z.ns, z.small, z.d),
+    )
+    n_items = 1 + z.m + 5
+    return pl.pallas_call(
+        functools.partial(front_kernel, z),
+        out_shape=outs,
+        in_specs=[VMEM] * 3 + [SMEM] + [VMEM] * 9,
+        out_specs=[VMEM] * len(outs),
+        scratch_shapes=[
+            pltpu.VMEM((z.slots, z.d), BF),
+            pltpu.VMEM((z.slots, z.d), BF),
+            pltpu.VMEM((8, HEADS * BUCKETS), F32),
+            pltpu.VMEM((z.m, z.t, z.g), I32),
+            pltpu.VMEM((z.m, z.t, z.g), F32),
+            pltpu.SemaphoreType.DMA((n_items, z.ns)),
+            pltpu.SemaphoreType.DMA((n_items, z.ns)),
+            pltpu.SemaphoreType.DMA((1, z.ne)),
+            pltpu.SemaphoreType.DMA((1, z.ne)),
+        ],
+        compiler_params=pltpu.CompilerParams(
+            collective_id=0, has_side_effects=True, vmem_limit_bytes=60 * 2**20
+        ),
+        name="front",
+    )(tokens, dy, routes, counts, wk, wv, wq, wo, small, perm, rows_of, dest, place_m)
+
+
+def small_block(z, own, w_router, gain_attn, gain_ffn, pos_table):
+    share = jnp.concatenate(
+        [w_router.T, gain_attn[None], gain_ffn[None], jnp.zeros((14, z.r), BF)], 0
+    )
+    col = jnp.arange(z.d)
+    wide = jnp.where(col[None] // z.r == own, jnp.tile(share, (1, z.ns)), 0)
+    n = pos_table.shape[0]
+    table = jnp.where(col // n == own, jnp.tile(pos_table, z.d // n), 0)
+    return jnp.where(jnp.arange(z.small)[:, None] == z.e + 2, table[None], wide)
+
+
+GELU_A = math.sqrt(2.0 / math.pi)
+GELU_B = 0.044715
+
+
+def expert_kernel(
+    z,
+    xs, dyg_in, w_in, w_out, perm, gate_of, source, pick,
+    ret, din, dout,
+    xr, xg, gwg, gwc, act, gp, dyg, part, rp, ysum, ry, fin,
+    csem, gsend, grecv, xsend, xrecv, psend, precv, ysend, yrecv, rsend, rrecv,
+):
+    p = Place(z)
+    load = pltpu.make_async_copy(dyg_in, dyg, csem.at[0])
+    load.start()
+    p.barrier()
+    t, d = z.t, z.d
+    half = d // 2
+    x_move = Exchange(
+        p,
+        lambda to: xs.at[aligned(to * z.sp, z.sp, 16)],
+        lambda at: xr.at[pl.ds(at * z.sp, z.sp)],
+        xsend,
+        xrecv,
+        0,
+    )
+    x_move.start(0)
+    x_move.start(1)
+    xr[0 : z.sp, :] = xs[aligned(p.e * z.sp, z.sp, 16), :]
+    load.wait()
+
+    tiles = z.ff // 256
+
+    def expert_rows(ref, h, l, cols):
+        return ref[:, aligned(h * z.cb + l * z.cr, z.cr, 16), cols].reshape(z.ns * z.cr, -1)
+
+    def gradient(i, carry):
+        h = lax.div(i, z.el * tiles)
+        l = lax.div(lax.rem(i, z.el * tiles), tiles)
+        at = aligned(lax.rem(i, tiles) * 256, 256, 256)
+        g = dot_t(expert_rows(dyg, h, l, slice(None)), w_out[l, at, :])
+        gp[:, aligned(h * z.cb + l * z.cr, z.cr, 16), at] = g.astype(BF).reshape(z.ns, z.cr, 256)
+        return carry
+
+    lax.fori_loop(0, 2 * z.el * tiles, gradient, 0)
+
+    def gather_of(h):
+        at = pl.ds(h * z.cb, z.cb)
+        return (
+            Gather(p, gwg.at[p.s, h], lambda o: gwg.at[o, h], gsend, grecv, 2 * h),
+            Gather(p, xg.at[p.s, at], lambda o: xg.at[o, at], gsend, grecv, 2 * h + 1),
+        )
+
+    gathers = [gather_of(h) for h in range(2)]
+
+    def distribute(h):
+        x_move.arrive(h)
+        rows_h = slice(h * z.hs, (h + 1) * z.hs)
+        gwg[p.s, h] = dot(gate_of[...], xr[rows_h, :LANES]).astype(BF)
+        gathers[h][0].start()
+
+        def order(i, carry):
+            cols = aligned(i * 256, 256, 256)
+            xg[p.s, h * z.cb : (h + 1) * z.cb, cols] = dot(perm[...], xr[rows_h, cols]).astype(BF)
+            return carry
+
+        lax.fori_loop(0, d // 256, order, 0)
+        gathers[h][1].start()
+
+    def collect(h, forward):
+        for item in gathers[h]:
+            if forward:
+                item.forward()
+            else:
+                item.arrive()
+
+    def gate_columns(h):
+        for b in range(z.ns):
+            wide = dot(source[...], gwg[b, h]) * pick[...].astype(F32)
+            gwc[b, h * z.cb : (h + 1) * z.cb, :] = jnp.sum(wide, axis=1, keepdims=True)
+
+    def activate(h):
+        gate_columns(h)
+
+        def step(i, carry):
+            l = lax.div(i, tiles)
+            at = aligned(lax.rem(i, tiles) * 256, 256, 256)
+            rows = aligned(h * z.cb + l * z.cr, z.cr, 16)
+            x = dot(expert_rows(xg, h, l, slice(None)), w_in[l, :, at])
+            g = expert_rows(gp, h, l, at).astype(F32)
+            gate = gwc[:, rows, :].reshape(z.ns * z.cr, 1)
+            x2 = x * x
+            th = jnp.tanh(x * (GELU_A + (GELU_A * GELU_B) * x2))
+            hx = 0.5 * x
+            up = 1.0 + th
+            act[:, rows, at] = (hx * up).astype(BF).reshape(z.ns, z.cr, 256)
+            slope = 0.5 * up + hx * (1.0 - th * th) * (GELU_A + (3.0 * GELU_A * GELU_B) * x2)
+            gp[:, rows, at] = (g * gate * slope).astype(BF).reshape(z.ns, z.cr, 256)
+            return carry
+
+        lax.fori_loop(0, z.el * tiles, step, 0)
+
+    def unit(kind, h, half_id):
+        return (kind * 2 + h) * 2 + half_id
+
+    partner = (p.e, p.shard(0, True))
+
+    def to_partner(u):
+        return rcopy(part.at[u, 1 - p.c], rp.at[u], psend.at[u], precv.at[u], partner)
+
+    def to_y(u, k):
+        return rcopy(
+            ysum.at[u, k - 1], ry.at[u, k - 1], ysend.at[u, k - 1], yrecv.at[u, k - 1], (p.e, p.shard(k, False))
+        )
+
+    def stage_a(kind, h, half_id):
+        u = unit(kind, h, half_id)
+        cols = slice(half_id * half, (half_id + 1) * half)
+
+        def step(l, carry):
+            if kind == 0:
+                out = dot_t(expert_rows(gp, h, l, slice(None)), w_in[l, cols, :])
+            else:
+                out = dot(expert_rows(act, h, l, slice(None)), w_out[l, :, cols])
+            out = out.astype(BF)
+            for b in range(z.ns):
+                part[u, b % 2, b // 2, aligned(l * z.cr, z.cr, 16), :] = out[b * z.cr : (b + 1) * z.cr]
+            return carry
+
+        lax.fori_loop(0, z.el, step, 0)
+        to_partner(u).start()
+
+    def stage_b(kind, h, half_id):
+        u = unit(kind, h, half_id)
+        to_partner(u).wait_recv()
+        for k in range(1, z.ny):
+            yy = lax.rem(p.y + k, z.ny)
+            ysum[u, k - 1] = (part[u, p.c, yy].astype(F32) + rp[u, yy].astype(F32)).astype(BF)
+            to_y(u, k).start()
+
+    def back(u, h, half_id, kind):
+        def copy(k):
+            cols = pl.ds(half_id * half, half)
+            away = (-k[0] % z.nz, k[1])
+            return rcopy(
+                fin.at[u, pl.ds((position(z, k) - h * z.hn) * z.sp, z.sp)],
+                ret.at[kind, aligned(p.e * z.sp, z.sp, 16), cols],
+                rsend.at[u, position(z, k) - h * z.hn],
+                rrecv.at[u, position(z, away) - h * z.hn],
+                (p.expert(*k), p.s),
+            )
+
+        def landing(k):
+            cols = pl.ds(half_id * half, half)
+            return rcopy(
+                fin.at[u, pl.ds((position(z, k) - h * z.hn) * z.sp, z.sp)],
+                ret.at[kind, aligned(p.expert(*k) * z.sp, z.sp, 16), cols],
+                rsend.at[u, position(z, k) - h * z.hn],
+                rrecv.at[u, position(z, k) - h * z.hn],
+                (p.expert(*k), p.s),
+            )
+
+        return copy, landing
+
+    def stage_c(kind, h, half_id):
+        u = unit(kind, h, half_id)
+        total = part[u, p.c, p.y].astype(F32) + rp[u, p.y].astype(F32)
+        for k in range(1, z.ny):
+            to_y(u, k).wait_recv()
+            total = total + ry[u, k - 1].astype(F32)
+        fin[u] = tdot(perm[...], total.astype(BF)).astype(BF)
+        copy, _ = back(u, h, half_id, kind)
+        for k in offsets(z, h):
+            copy(k).start()
+        if h == 0:
+            cols = slice(half_id * half, (half_id + 1) * half)
+            ret[kind, aligned(p.e * z.sp, z.sp, 16), cols] = fin[u, 0 : z.sp, :]
+
+    def stage_d(kind, h, half_id):
+        u = unit(kind, h, half_id)
+        copy, landing = back(u, h, half_id, kind)
+        for k in offsets(z, h):
+            landing(k).wait_recv()
+        for k in offsets(z, h):
+            copy(k).wait_send()
+        to_partner(u).wait_send()
+        for k in range(1, z.ny):
+            to_y(u, k).wait_send()
+
+    def weights(l):
+        def gate_dy(i, carry):
+            rows = aligned(lax.div(i, 2) * z.cb + l * z.cr, z.cr, 16)
+            cols = aligned(lax.rem(i, 2) * half, half, LANES)
+            dyg[:, rows, cols] = (dyg[:, rows, cols].astype(F32) * gwc[:, rows, :]).astype(BF)
+            return carry
+
+        lax.fori_loop(0, 4, gate_dy, 0)
+
+        def both(ref, cols):
+            return jnp.concatenate([expert_rows(ref, h, l, cols) for h in range(2)], 0)
+
+        def step(i, carry):
+            at = aligned(i * 256, 256, 256)
+            dout[l, :, at] = tdot(both(act, slice(None)), both(dyg, at)).astype(BF)
+            return carry
+
+        lax.fori_loop(0, d // 256, step, 0)
+
+        def step_in(i, carry):
+            at = aligned(i * 256, 256, 256)
+            din[l, :, at] = tdot(both(xg, slice(None)), both(gp, at)).astype(BF)
+            return carry
+
+        lax.fori_loop(0, tiles, step_in, 0)
+
+    distribute(0)
+    distribute(1)
+    collect(0, True)
+    collect(0, False)
+    activate(0)
+    stage_a(0, 0, 0)
+    stage_a(0, 0, 1)
+    stage_b(0, 0, 0)
+    stage_b(0, 0, 1)
+    collect(1, True)
+    collect(1, False)
+    activate(1)
+    stage_a(0, 1, 0)
+    stage_c(0, 0, 0)
+    stage_b(0, 1, 0)
+    stage_a(0, 1, 1)
+    stage_c(0, 0, 1)
+    stage_b(0, 1, 1)
+    stage_a(1, 0, 0)
+    stage_a(1, 0, 1)
+    stage_b(1, 0, 0)
+    stage_b(1, 0, 1)
+    stage_a(1, 1, 0)
+    stage_a(1, 1, 1)
+    stage_c(0, 1, 0)
+    stage_b(1, 1, 0)
+    stage_b(1, 1, 1)
+    stage_c(0, 1, 1)
+    weights(0)
+    stage_c(1, 0, 0)
+    stage_c(1, 0, 1)
+    weights(1)
+    stage_c(1, 1, 0)
+    stage_c(1, 1, 1)
+    for kind in range(2):
+        for h in range(2):
+            for half_id in range(2):
+                stage_d(kind, h, half_id)
+    x_move.finish()
+    for pair in gathers:
+        for item in pair:
+            item.finish()
+
+
+def experts(z, xs, dyg, w_in, w_out, perm, gate_of, source, pick):
+    def bf(*shape):
+        return jax.ShapeDtypeStruct(shape, BF)
+
+    dma = pltpu.SemaphoreType.DMA
+    half = z.d // 2
+    return pl.pallas_call(
+        functools.partial(expert_kernel, z),
+        out_shape=(bf(2, z.slots, z.d), bf(z.el, z.d, z.ff), bf(z.el, z.ff, z.d)),
+        in_specs=[VMEM, pl.BlockSpec(memory_space=pl.ANY)] + [VMEM] * 6,
+        out_specs=[VMEM] * 3,
+        scratch_shapes=[
+            pltpu.VMEM((z.slots, z.d), BF),
+            pltpu.VMEM((z.ns, z.blk, z.d), BF),
+            pltpu.VMEM((z.ns, 2, 2 * z.n16, LANES), BF),
+            pltpu.VMEM((z.ns, z.blk, 1), F32),
+            pltpu.VMEM((z.ns, z.blk, z.ff), BF),
+            pltpu.VMEM((z.ns, z.blk, z.ff), BF),
+            pltpu.VMEM((z.ns, z.blk, z.d), BF),
+            pltpu.VMEM((8, 2, z.ny, z.cb, half), BF),
+            pltpu.VMEM((8, z.ny, z.cb, half), BF),
+            pltpu.VMEM((8, z.ny - 1, z.cb, half), BF),
+            pltpu.VMEM((8, z.ny - 1, z.cb, half), BF),
+            pltpu.VMEM((8, z.hs, half), BF),
+            dma((1,)),
+            dma((4, z.ns)), dma((4, z.ns)),
+            dma((1, z.ne)), dma((1, z.ne)),
+            dma((8,)), dma((8,)),
+            dma((8, z.ny)), dma((8, z.ny)),
+            dma((8, z.hn)), dma((8, z.hn)),
+        ],
+        compiler_params=pltpu.CompilerParams(
+            collective_id=1, has_side_effects=True, vmem_limit_bytes=60 * 2**20
+        ),
+        name="experts",
+    )(xs, dyg, w_in, w_out, perm, gate_of, source, pick)
+
+
+class Scatter:
+    def __init__(self, place, part, from_core, to_y, from_y, psend, precv, ysend, yrecv):
+        self.p, self.part, self.from_core = place, part, from_core
+        self.to_y, self.from_y = to_y, from_y
+        self.psend, self.precv, self.ysend, self.yrecv = psend, precv, ysend, yrecv
+
+    def core_copy(self):
+        p = self.p
+        return rcopy(
+            self.part.at[1 - p.c], self.from_core, self.psend, self.precv, (p.e, p.shard(0, True))
+        )
+
+    def y_copy(self, k):
+        p = self.p
+        return rcopy(
+            self.to_y.at[k - 1], self.from_y.at[k - 1], self.ysend.at[k - 1], self.yrecv.at[k - 1],
+            (p.e, p.shard(k, False)),
+        )
+
+    def send(self):
+        self.core_copy().start()
+
+    def middle(self):
+        p = self.p
+        self.core_copy().wait_recv()
+        for k in range(1, p.z.ny):
+            yy = lax.rem(p.y + k, p.z.ny)
+            both = self.part[p.c, yy].astype(F32) + self.from_core[yy].astype(F32)
+            self.to_y[k - 1] = both.astype(BF)
+            self.y_copy(k).start()
+
+    def total(self):
+        p = self.p
+        out = self.part[p.c, p.y].astype(F32) + self.from_core[p.y].astype(F32)
+        for k in range(1, p.z.ny):
+            self.y_copy(k).wait_recv()
+            out = out + self.from_y[k - 1].astype(F32)
+        return out
+
+    def finish(self):
+        self.core_copy().wait_send()
+        for k in range(1, self.p.z.ny):
+            self.y_copy(k).wait_send()
+
+
+class Sum:
+    def __init__(self, place, own, xin, xsum, zin, done, sems):
+        self.p, self.own, self.xin, self.xsum, self.zin, self.done = place, own, xin, xsum, zin, done
+        self.sx, self.rx, self.sz, self.rz, self.sg, self.rg, self.sh, self.rh = sems
+        self.rows, self.cols = own.shape
+        self.nz = place.z.nz
+        self.x, self.zz = lax.rem(place.e, 2), lax.div(place.e, 2)
+
+    def half(self, x):
+        return aligned(x * (self.cols // 2), self.cols // 2, LANES)
+
+    def piece(self, zz):
+        return aligned(zz * (self.rows // self.nz), self.rows // self.nz, 16)
+
+    def other_x(self):
+        return (self.p.expert(0, 1), self.p.s)
+
+    def other_z(self, k):
+        return (self.p.expert(k, 0), self.p.s)
+
+    def z_at(self, k):
+        return lax.rem(self.zz + k, self.nz)
+
+    def copy_x(self):
+        return rcopy(self.own.at[:, self.half(1 - self.x)], self.xin, self.sx, self.rx, self.other_x())
+
+    def copy_z(self, k):
+        return rcopy(
+            self.xsum.at[self.piece(self.z_at(k))], self.zin.at[k - 1], self.sz.at[k - 1], self.rz.at[k - 1],
+            self.other_z(k),
+        )
+
+    def copy_g(self, k, origin):
+        block = self.done.at[self.piece(origin), self.half(self.x)]
+        return rcopy(block, block, self.sg.at[k - 1], self.rg.at[k - 1], self.other_z(k))
+
+    def copy_h(self, x):
+        block = self.done.at[:, self.half(x)]
+        return rcopy(block, block, self.sh, self.rh, self.other_x())
+
+    def one(self):
+        self.copy_x().start()
+
+    def two(self):
+        self.copy_x().wait_recv()
+        self.xsum[...] = (self.own[:, self.half(self.x)].astype(F32) + self.xin[...].astype(F32)).astype(BF)
+        for k in range(1, self.nz):
+            self.copy_z(k).start()
+
+    def three(self):
+        out = self.xsum[self.piece(self.zz), :].astype(F32)
+        for k in range(1, self.nz):
+            self.copy_z(k).wait_recv()
+            out = out + self.zin[k - 1].astype(F32)
+        self.done[self.piece(self.zz), self.half(self.x)] = out.astype(BF)
+        for k in range(1, self.nz):
+            self.copy_g(k, self.zz).start()
+
+    def four(self):
+        for k in range(1, self.nz):
+            self.copy_g(k, self.z_at(self.nz - k)).wait_recv()
+        self.copy_h(self.x).start()
+
+    def five(self):
+        self.copy_h(1 - self.x).wait_recv()
+
+    def finish(self):
+        self.copy_x().wait_send()
+        for k in range(1, self.nz):
+            self.copy_z(k).wait_send()
+            self.copy_g(k, self.zz).wait_send()
+        self.copy_h(self.x).wait_send()
+
+
+def back_kernel(
+    z,
+    dy, routes, counts, toks, hid, kk, vv, qq, pp, ctx, mid, nrm, sd, smallg, fk, fv, fq, fo, ret,
+    mixed, dtok, dq, dk, dv, do, dsmall,
+    gctx, gqb, gkb, gvb, gmid, lower, edge_id, edge_ok, tab, gain_rows,
+    wpart, wrp, wys, wyr, wsum, wxin, wxs, wzin, wdone,
+    gpart, grp, gys, gyr, sbuf, sone, stwo, sthree, sfour,
+    wp1, wp2, wy1, wy2, ux1, ux2, uz1, uz2, ug1, ug2, uh1, uh2, gp1, gp2, gy1, gy2, ss1, ss2,
+):
+    p = Place(z)
+    p.barrier()
+    t, d, mt = z.t, z.d, z.mt
+    sums = smallg[0].astype(F32)
+    for b in range(1, z.ns):
+        sums = sums + smallg[b].astype(F32)
+    gain_one = sums[z.e : z.e + 1, :]
+    gain_two = sums[z.e + 1 : z.e + 2, :]
+    router = sums.astype(BF)
+
+    slot0, slot1 = sd[:, 0:1], sd[:, 1:2]
+    gate0, gate1 = sd[:, 2:3], sd[:, 3:4]
+    hot0, hot1 = one_hot(z, slot0).astype(BF), one_hot(z, slot1).astype(BF)
+    grad = dy[...].astype(F32)
+    first, second = dot(hot0, ret[1]), dot(hot1, ret[1])
+    mixed[...] = (mid[...] + gate0 * first + gate1 * second).astype(BF)
+    toward0 = jnp.sum(grad * first, axis=1, keepdims=True)
+    toward1 = jnp.sum(grad * second, axis=1, keepdims=True)
+    mean = gate0 * toward0 + gate1 * toward1
+    lane = iota((mt, z.small), 1)
+    glog = jnp.where(lane == routes[:, 0:1], gate0 * (toward0 - mean), 0.0)
+    glog = (glog + jnp.where(lane == routes[:, 1:2], gate1 * (toward1 - mean), 0.0)).astype(BF)
+    gnorm = dot(glog, router) + dot(hot0, ret[0]) + dot(hot1, ret[0])
+    x = mid[...]
+    scale = lax.rsqrt(jnp.mean(x * x, axis=1, keepdims=True) + EPS)
+    xh = x * scale
+    gain_rows[1:2, :] = jnp.sum(gnorm * xh, axis=0, keepdims=True)
+    gy = gnorm * gain_two
+    gm = grad + scale * (gy - xh * jnp.mean(gy * xh, axis=1, keepdims=True))
+    gmid[...] = gm
+    gattn = gm.astype(BF)
+    sbuf[...] = tdot(glog, nrm[...])
+
+    def reduction(u):
+        shard_sum = Scatter(
+            p, wpart.at[u], wrp.at[u], wys.at[u], wyr.at[u], wp1.at[u], wp2.at[u], wy1.at[u], wy2.at[u]
+        )
+        expert_sum = Sum(
+            p, wsum.at[u], wxin.at[u], wxs.at[u], wzin.at[u], wdone.at[u],
+            (ux1.at[u], ux2.at[u], uz1.at[u], uz2.at[u], ug1.at[u], ug2.at[u], uh1.at[u], uh2.at[u]),
+        )
+        return shard_sum, expert_sum
+
+    pairs = [reduction(u) for u in range(4)]
+
+    def stage(u, n):
+        shard_sum, expert_sum = pairs[u]
+        if n == 0:
+            shard_sum.send()
+        elif n == 1:
+            shard_sum.middle()
+        elif n == 2:
+            wsum[u] = shard_sum.total().astype(BF)
+            expert_sum.one()
+        elif n == 3:
+            expert_sum.two()
+        elif n == 4:
+            expert_sum.three()
+        elif n == 5:
+            expert_sum.four()
+        else:
+            expert_sum.five()
+
+    def put(u, cols, value):
+        value = value.astype(BF)
+        for b in range(z.ns):
+            wpart[u, b % 2, b // 2, :, cols] = value[b * z.r : (b + 1) * z.r]
+
+    for i in range(d // 256):
+        cols = slice(i * 256, (i + 1) * 256)
+        put(3, cols, tdot(ctx[...], gattn[:, cols]))
+    stage(3, 0)
+    for i in range(d // 256):
+        cols = slice(i * 256, (i + 1) * 256)
+        gctx[:, cols] = dot_t(gattn, fo[cols, :]).astype(BF)
+
+    tab[...] = jnp.zeros_like(tab)
+    lane = iota((1, LANES), 1)
+    starts = jnp.where(lane <= 16, lane, 0)
+    for i, edge in enumerate(BUCKET_EDGES):
+        starts = jnp.where(lane == 17 + i, edge, starts)
+    for m in range(z.m):
+        key_pos, _ = key_layout(z, counts, m, (z.g, 1), 0)
+        lower[m] = jnp.where(key_pos <= iota((z.g, z.far), 1), 1.0, 0.0).astype(BF)
+        at = query_position(z, counts, m, p.s) - starts
+        ok = (at >= 0) & (lane < BUCKETS)
+        edge_id[m] = jnp.where(ok, at, 0)
+        edge_ok[m] = jnp.where(ok, 1.0, 0.0)
+    low = iota((t, LANES), 1) < 64
+
+    def attend_back(i, unit):
+        m = lax.rem(i, z.m)
+        pair = unit * 2 + lax.div(i, z.m)
+        cols = aligned(pair * LANES, LANES, LANES)
+        rows = aligned(m * t, t, 16)
+        q, g = qq[rows, cols], gctx[rows, cols]
+        zero = jnp.zeros_like(q)
+        q_two = jnp.concatenate([jnp.where(low, q, zero), jnp.where(low, zero, q)], 0)
+        g_two = jnp.concatenate([jnp.where(low, g, zero), jnp.where(low, zero, g)], 0)
+        probs = pp[m * z.pairs + pair]
+        pf = probs.astype(F32)
+        gp = dot_t(g_two, vv[m, :, cols])
+        gs = (pf * (gp - jnp.sum(pf * gp, axis=1, keepdims=True))).astype(BF)
+        two = dot(gs, kk[m, :, cols])
+        gqb[rows, cols] = (jnp.where(low, two[:t], two[t:]) * 0.125).astype(BF)
+        gkb[m, :, cols] = tdot(gs, q_two).astype(BF)
+        gvb[m, :, cols] = tdot(probs, g_two).astype(BF)
+        total = dot(gs, lower[m])
+        for half in range(2):
+            found = jnp.zeros((t, LANES), F32)
+            for b in range(z.far // LANES):
+                at = edge_id[m] - b * LANES
+                inside = (at >= 0) & (at < LANES)
+                got = jnp.take_along_axis(
+                    total[half * t : (half + 1) * t, b * LANES : (b + 1) * LANES], jnp.where(inside, at, 0), axis=1
+                )
+                found = jnp.where(inside, got, found)
+            found = jnp.sum(found * edge_ok[m], axis=0, keepdims=True)
+            row = pl.ds(pair * 2 + half, 1)
+            tab[row, :] = tab[row, :] + found
+        return unit
+
+    def attention(unit):
+        lax.fori_loop(0, z.m * 2, attend_back, unit)
+
+    def own_hidden():
+        return jnp.concatenate([hid[m, aligned(p.s * t, t, 16), :] for m in range(z.m)], 0)
+
+    def weight_grads(u):
+        cols = slice(u * 256, (u + 1) * 256)
+        put(u, slice(0, 256), tdot(own_hidden(), gqb[:, cols]))
+        every = hid[...].reshape(z.m * z.g, d)
+        put(u, slice(256, 512), tdot(every, gkb[:, :, cols].reshape(z.m * z.g, 256)))
+        put(u, slice(512, 768), tdot(every, gvb[:, :, cols].reshape(z.m * z.g, 256)))
+
+    grads = [
+        Scatter(p, gpart.at[m], grp.at[m], gys.at[m], gyr.at[m], gp1.at[m], gp2.at[m], gy1.at[m], gy2.at[m])
+        for m in range(z.m)
+    ]
+
+    def hidden_grads(m):
+        for b in range(z.ns):
+            rows = slice(b * t, (b + 1) * t)
+            gh = dot_t(gkb[m, rows, :], fk[...]) + dot_t(gvb[m, rows, :], fv[...])
+            mine = jnp.where(p.s == b, 1.0, 0.0)
+            gh = gh + mine * dot_t(gqb[m * t : (m + 1) * t, :], fq[...])
+            gpart[m, b % 2, b // 2] = gh.astype(BF)
+            x = toks[m, rows, :].astype(F32)
+            scale = lax.rsqrt(jnp.mean(x * x, axis=1, keepdims=True) + EPS)
+            row = jnp.sum(gh * x * scale, axis=0, keepdims=True)
+            if m == 0 and b == 0:
+                gain_rows[0:1, :] = row
+            else:
+                gain_rows[0:1, :] = gain_rows[0:1, :] + row
+
+    def token_grads(m):
+        gh = grads[m].total()
+        rows = slice(m * t, (m + 1) * t)
+        x = toks[m, aligned(p.s * t, t, 16), :].astype(F32)
+        scale = lax.rsqrt(jnp.mean(x * x, axis=1, keepdims=True) + EPS)
+        xh = x * scale
+        gy = gh * gain_one
+        dtok[rows, :] = gmid[rows, :] + scale * (gy - xh * jnp.mean(gy * xh, axis=1, keepdims=True))
+
+    nz = z.nz
+
+    def small_copy(n, k=0):
+        if n == 0:
+            return rcopy(sone.at[0], sone.at[1], ss1.at[0], ss2.at[0], (p.e, p.shard(0, True)))
+        if n == 1:
+            return rcopy(stwo.at[0], stwo.at[k], ss1.at[k], ss2.at[k], (p.e, p.shard(k, False)))
+        if n == 2:
+            return rcopy(sthree.at[0], sthree.at[1], ss1.at[z.ny], ss2.at[z.ny], (p.expert(0, 1), p.s))
+        zz = lax.div(p.e, 2)
+        return rcopy(sfour.at[zz], sfour.at[zz], ss1.at[z.ny + k], ss2.at[z.ny + k], (p.expert(k, 0), p.s))
+
+    def small_pack():
+        tabs = tab[...]
+        tabs = tabs - pltpu.roll(tabs, LANES - 1, 1)
+        lane16 = iota(tabs.shape, 1)
+        tabs = jnp.where(lane16 < BUCKETS, tabs, 0.0)
+        row = iota(sbuf.shape, 0)
+        out = sbuf[...]
+        out = jnp.where(row == z.e, gain_rows[0:1, :], out)
+        out = jnp.where(row == z.e + 1, gain_rows[1:2, :], out)
+        sbuf[...] = out
+        line = []
+        per = LANES // BUCKETS
+        for c in range(HEADS // per):
+            piece = tabs[c * per : c * per + 1, :]
+            for j in range(1, per):
+                piece = piece + pltpu.roll(tabs[c * per + j : c * per + j + 1, :], j * BUCKETS, 1)
+            line.append(piece)
+        for c, piece in enumerate(line):
+            sbuf[z.e + 2 : z.e + 3, c * LANES : (c + 1) * LANES] = piece
+        sone[0] = sbuf[...].astype(BF)
+        small_copy(0).start()
+
+    def small_step(n):
+        if n == 1:
+            small_copy(0).wait_recv()
+            stwo[0] = (sone[0].astype(F32) + sone[1].astype(F32)).astype(BF)
+            for k in range(1, z.ny):
+                small_copy(1, k).start()
+        elif n == 2:
+            out = stwo[0].astype(F32)
+            for k in range(1, z.ny):
+                small_copy(1, k).wait_recv()
+                out = out + stwo[k].astype(F32)
+            sthree[0] = out.astype(BF)
+            small_copy(2).start()
+        elif n == 3:
+            small_copy(2).wait_recv()
+            sfour[lax.div(p.e, 2)] = (sthree[0].astype(F32) + sthree[1].astype(F32)).astype(BF)
+            for k in range(1, nz):
+                small_copy(3, k).start()
+        else:
+            for k in range(1, nz):
+                small_copy(3, k).wait_recv()
+            out = sfour[0].astype(F32)
+            for k in range(1, nz):
+                out = out + sfour[k].astype(F32)
+            dsmall[...] = out
+
+    attention(0)
+    stage(3, 1)
+    weight_grads(0)
+    stage(0, 0)
+    stage(3, 2)
+    attention(1)
+    stage(0, 1)
+    stage(3, 3)
+    weight_grads(1)
+    stage(1, 0)
+    stage(0, 2)
+    stage(3, 4)
+    attention(2)
+    stage(1, 1)
+    stage(0, 3)
+    stage(3, 5)
+    weight_grads(2)
+    stage(2, 0)
+    stage(1, 2)
+    stage(0, 4)
+    hidden_grads(0)
+    grads[0].send()
+    stage(2, 1)
+    stage(1, 3)
+    stage(0, 5)
+    hidden_grads(1)
+    grads[1].send()
+    grads[0].middle()
+    small_pack()
+    stage(2, 2)
+    stage(1, 4)
+    grads[1].middle()
+    small_step(1)
+    token_grads(0)
+    stage(2, 3)
+    stage(1, 5)
+    small_step(2)
+    token_grads(1)
+    small_step(3)
+    stage(2, 4)
+    small_step(4)
+    stage(2, 5)
+    for u in (3, 0, 1, 2):
+        stage(u, 6)
+        if u == 3:
+            do[...] = wdone[3].astype(F32)
+        else:
+            cols = slice(u * 256, (u + 1) * 256)
+            dq[:, cols] = wdone[u, :, 0:256].astype(F32)
+            dk[:, cols] = wdone[u, :, 256:512].astype(F32)
+            dv[:, cols] = wdone[u, :, 512:768].astype(F32)
+    for shard_sum, expert_sum in pairs:
+        shard_sum.finish()
+        expert_sum.finish()
+    for item in grads:
+        item.finish()
+    small_copy(0).wait_send()
+    for k in range(1, z.ny):
+        small_copy(1, k).wait_send()
+    small_copy(2).wait_send()
+    for k in range(1, nz):
+        small_copy(3, k).wait_send()
+
+
+def back(z, *inputs):
+    def bf(*shape):
+        return pltpu.VMEM(shape, BF)
+
+    def f32(*shape):
+        return jax.ShapeDtypeStruct(shape, F32)
+
+    dma = pltpu.SemaphoreType.DMA
+    d, r, ny, nz = z.d, z.r, z.ny, z.nz
+    n_small = z.ny + z.nz
+    outs = (
+        jax.ShapeDtypeStruct((z.mt, d), BF), f32(z.mt, d),
+        f32(r, d), f32(r, d), f32(r, d), f32(r, d), f32(z.small, d),
+    )
+    return pl.pallas_call(
+        functools.partial(back_kernel, z),
+        out_shape=outs,
+        in_specs=[VMEM] * 2 + [SMEM] + [VMEM] * 16,
+        out_specs=[VMEM] * len(outs),
+        scratch_shapes=[
+            bf(z.mt, d), bf(z.mt, d), bf(z.m, z.g, d), bf(z.m, z.g, d), pltpu.VMEM((z.mt, d), F32),
+            bf(z.m, z.g, z.far), pltpu.VMEM((z.m, z.t, LANES), I32), pltpu.VMEM((z.m, z.t, LANES), F32),
+            pltpu.VMEM((16, LANES), F32), pltpu.VMEM((8, d), F32),
+            bf(4, 2, ny, r, d), bf(4, ny, r, d), bf(4, ny - 1, r, d), bf(4, ny - 1, r, d),
+            bf(4, r, d), bf(4, r, d // 2), bf(4, r, d // 2), bf(4, nz - 1, r // nz, d // 2), bf(4, r, d),
+            bf(z.m, 2, ny, z.t, d), bf(z.m, ny, z.t, d), bf(z.m, ny - 1, z.t, d), bf(z.m, ny - 1, z.t, d),
+            pltpu.VMEM((z.small, d), F32), bf(2, z.small, d), bf(ny, z.small, d), bf(2, z.small, d),
+            bf(nz, z.small, d),
+            dma((4,)), dma((4,)), dma((4, ny)), dma((4, ny)),
+            dma((4,)), dma((4,)), dma((4, nz)), dma((4, nz)), dma((4, nz)), dma((4, nz)), dma((4,)), dma((4,)),
+            dma((z.m,)), dma((z.m,)), dma((z.m, ny)), dma((z.m, ny)),
+            dma((n_small,)), dma((n_small,)),
+        ],
+        compiler_params=pltpu.CompilerParams(
+            collective_id=2, has_side_effects=True, vmem_limit_bytes=60 * 2**20
+        ),
+        name="back",
+    )(*inputs)
+
+
+def fused_device(
+    z, tokens, cotangent, routes, prompt_rows, w_query, w_key, w_value, w_output, w_router, gain_attn, gain_ffn,
+    pos_table, w_in, w_out,
+):
+    own = lax.axis_index("shard")
+    perm, rows_of, dest, place, gate_of, source, pick = layout_constants(z)
+    small = small_block(z, own, w_router, gain_attn, gain_ffn, pos_table)
+    dy = cotangent.reshape(z.mt, z.d)
+    routes = routes.reshape(z.mt, 2)
+    counts = prompt_rows[:, 0]
+    toks, hid, kk, vv, qq, pp, ctx, mid, nrm, sd, xs, dyg, fk, fv, fq, fo, smallg = front(
+        z, tokens, dy, routes, counts, w_key, w_value, w_query, w_output, small, perm, rows_of, dest, place
+    )
+    ret, din, dout = experts(z, xs, dyg, w_in, w_out, perm, gate_of, source, pick)
+    mixed, dtok, dq, dk, dv, do, dsmall = back(
+        z, dy, routes, counts, toks, hid, kk, vv, qq, pp, ctx, mid, nrm, sd, smallg, fk, fv, fq, fo, ret
+    )
+    share = lax.dynamic_slice_in_dim(dsmall, own * z.r, z.r, axis=1)
+    n = pos_table.shape[0]
+    return (
+        mixed.reshape(tokens.shape),
+        dtok.reshape(tokens.shape),
+        dq,
+        dk,
+        dv,
+        do,
+        share[: z.e].T,
+        share[z.e],
+        share[z.e + 1],
+        lax.dynamic_slice_in_dim(dsmall[z.e + 2], own * n, n),
+        din.astype(F32),
+        dout.astype(F32),
+    )
+
+
 HIGHEST = lax.Precision.HIGHEST
 
 
@@ -470,6 +1779,15 @@
         P("expert", None, "shard"),
         P("expert", "shard", None),
     )
+    ne, ns = mesh.shape["expert"], mesh.shape["shard"]
+
+    def device(*args):
+        tokens, w_router, w_in = args[0], args[8], args[12]
+        z = Sizes(
+            ne, ns, tokens.shape[0], tokens.shape[1], tokens.shape[2], w_router.shape[1], w_in.shape[0], w_in.shape[2]
+        )
+        return fused_device(z, *args) if z.fits() else per_device(*args)
+
     return jax.shard_map(
-        per_device, mesh=mesh, in_specs=in_specs, out_specs=out_specs, check_vma=False
-    )
+        device, mesh=mesh, in_specs=in_specs, out_specs=out_specs, check_vma=False
+    )

time: 885 us -> 277 us (0.31)
  waiting for transfers between devices: 366 us -> 0 us
  Pallas kernels: 0 us -> 256 us
  matrix products: 194 us -> 0 us
  blocking collectives: 96.7 us -> 0 us
  local copies, waits for them, and re-layouts: 105 us -> 12.8 us
  other arithmetic: 56 us -> 6.6 us
  starting transfers between devices: 42.5 us -> 0 us
  between operations: 19.1 us -> 0.72 us
    pallas_call x0 -> x3, Pallas kernels: none -> 256 us  [the longest x1 96.4 us: experts(): pl.pallas_call(functools.partial(expert_kernel, z), out_shape=(bf(2, z.sl...]
    reduce_scatter x6 -> x0, waiting for transfers between devices: 244 us -> none  [the longest x1 76.9 us: per_device(): lax.psum_scatter(sum_expert_in.astype(jnp.bfloat16), 'shard', scatter_dim...]
    dot_general x58 -> x0, matrix products: 194 us -> none  [the longest x2 25.5 us: per_device(): jnp.einsum('ref,red->efd', activation, grad_recv, preferred_element_type=...]
    all_gather x5 -> x0, blocking collectives: 59.1 us -> none  [the longest x2 27 us: per_device(): lax.all_gather(key, 'shard', axis=0, tiled=True)]
    unnamed x23 -> x0, waiting for transfers between devices: 58.6 us -> none
    all_to_all x8 -> x0, starting transfers between devices: 41.2 us -> none  [the longest x2 12.3 us: per_device(): lax.all_to_all(grad_in_low, 'expert', split_axis=0, concat_axis=0, tiled=...]
    gather x16 -> x0, local copies, waits for them, and re-layouts: 32.3 us -> none  [the longest x2 6.97 us: per_device(): key_pos = pos_all[key_index]]
    all_to_all x8 -> x0, waiting for transfers between devices: 31.8 us -> none  [the longest x2 16.9 us: per_device(): lax.all_to_all(grad_in_low, 'expert', split_axis=0, concat_axis=0, tiled=...]
  transfers between devices with their start and end apart: 26 -> 0, of which waited for: 15 -> 0; matrix products, arithmetic and copies ran while one was open for 36% -> 0% of each run, Pallas kernels for 0% -> 0%
where the time goes in v1:
time: 277 us; the launch traced here: 276 us
  Pallas kernels  256 us (92%)
  local copies, waits for them, and re-layouts  12.8 us (5%)
  other arithmetic  6.6 us (2%)
    pallas_call x1, Pallas kernels, experts(): pl.pallas_call(functools.partial(expert_kernel, z), out_shape=(bf(2, z.sl...  96.4 us
    pallas_call x1, Pallas kernels, back(): pl.pallas_call(functools.partial(back_kernel, z), out_shape=outs, in_spec...  83.4 us
    pallas_call x1, Pallas kernels, front(): pl.pallas_call(functools.partial(front_kernel, z), out_shape=outs, in_spe...  76.5 us
    unnamed x23, local copies, waits for them, and re-layouts  6.39 us

profile of v1, /device:TPU:0, one launch (start us, length us, event | category | flops | bytes accessed | tf_op | source)
XLA Modules:
  0.0 276.4 jit_solution(15106841982831079197)
XLA Ops:
  0.6 1.5 copy.33
  2.1 0.7 broadcast_in_dim.49
  2.8 0.7 broadcast_in_dim.48
  3.4 0.1 pad.3.clone
  3.5 0.8 maximum_maximum_fusion
  4.3 0.1 tile.21
  4.5 0.7 tile.8
  5.1 0.1 tile.9
  5.2 0.7 select_select_fusion.small
  5.9 76.5 %front.1 = (bf16[2,512,768]{2,1,0:T(8,128)(2,1)}, bf16[2,512,768]{2,1,0:T(8,128)(2,1)}, bf16[2,512,768]{2,1,0:T(8,128)(2,1)}, bf16[2,512,768]{2,1,0:T(8,128)(2,1...) custom-call(bf16[2,128,768]{2,1,0:T(8,128)(2,1)} %tokens.1, ...), custom_call_target="tpu_custom_call" | custom-call | tf_op jit(solution)/shard_map/front/pallas_call | solution.py:504
  82.5 96.4 %experts.1 = (bf16[2,640,768]{2,1,0:T(8,128)(2,1)}, bf16[2,768,768]{2,1,0:T(8,128)(2,1)}, bf16[2,768,768]{2,1,0:T(8,128)(2,1)}) custom-call(bf16[640,768]{1,0:T(8,128)(2,1)} %get-tuple-element.54.xs, bf16[4,576,768]{2,1,0:T(8,128)(2,1)} %get-tuple-element.55.dyg_in, bf16[2,768,768]{2,1,0:T(8,128)(2,1)} %w_in.1, bf16[2,768,768]{2,1,0:T(8,128)(2,1)} %w_out.1, ...), custom_call_target="tpu_custom_call" | custom-call | tf_op jit(solution)/shard_map/experts/pallas_call | solution.py:802
  178.8 0.0 copy-start.1
  178.9 83.4 %back.1 = (bf16[256,768]{1,0:T(8,128)(2,1)}, f32[256,768]{1,0:T(8,128)}, f32[192,768]{1,0:T(8,128)}, f32[192,768]{1,0:T(8,128)}, f32[192,768]{1,0:T(8,128)}, /*index=5*/f32[192,768]{1,0:T(8,128)}, f32[32,768]{1,0:T(8,128)}) custom-call(bf16[256,768]{1,0:T(8,128)(2,1)} %bitcast.13, s32[256,2]{1,0:T(8,128)} %bitcast.15, s32[2,4]{1,0:T(2,128)} %bitcast.20, ...), custom_call_target="tpu_custom_call" | custom-call | tf_op jit(solution)/shard_map/back/pallas_call | solution.py:1264
  262.2 1.4 dynamic-slice_bitcast_fusion
  263.7 1.4 fusion.8
  265.1 0.7 slice.15
  265.8 0.6 dynamic-slice_bitcast_fusion.1
  266.4 0.0 copy-done.1
  266.4 0.0 copy-start
  266.4 2.5 convert_element_type.10
  269.0 0.0 copy-done
  269.0 0.0 copy-start.7
  269.0 0.0 copy-start.2
  269.0 2.5 convert_element_type.11
  271.5 0.0 copy-done.7
  271.5 0.0 copy-start.6
  271.5 0.0 copy-start.5
  271.5 0.7 copy.40
  272.3 0.0 copy-done.2
  272.3 0.0 copy-start.4
  272.3 0.9 copy.41
  273.1 0.0 copy-done.6
  273.2 0.0 copy-start.3
  273.2 0.8 copy.42
  274.0 0.0 copy-done.5
  274.0 0.8 copy.43
  274.8 0.0 copy-done.4
  274.8 0.8 copy.44
  275.6 0.0 copy-done.3
  275.6 0.8 copy.45
  (5 shorter events, 0.1 us)
Async XLA Ops:
  178.8 87.6 %copy-start.1 = (bf16[2,768,768]{2,1,0:T(8,128)(2,1)S(1)}, bf16[2,768,768]{2,1,0:T(8,128)(2,1)}, u32[]{:S(2)}) copy-start(bf16[2,768,768]{2,1,0:T(8,128)(2,1)} %get-tuple-element.64) | copy-start | bytes 7077892
  266.4 2.6 copy-start
  269.0 2.6 copy-start.7
  269.0 3.3 %copy-start.2 = (f32[256,768]{1,0:T(8,128)S(1)}, f32[256,768]{1,0:T(8,128)}, u32[]{:S(2)}) copy-start(f32[256,768]{1,0:T(8,128)} %get-tuple-element.58) | copy-start | bytes 2359300
  271.5 1.6 copy-start.6
  271.5 2.5 copy-start.5
  272.3 2.5 copy-start.4
  273.2 2.5 copy-start.3
